TPU v7x, 32 devices: a whole 2x2x4 slice. The times are simulated.
32 devices in a mesh: grp: 2 (over x), row: 16 (over z, y, core).
Axes of the slice: x: 2, y: 2, z: 4, core: 2. Of those that a mesh axis runs over, the one named last changes fastest.
Arguments:
- object_slices: float32 [2, 2, 2048, 2048], P(None, None, ('grp', 'row')), parts along dimension 2
- probe_modes: float32 [8, 2, 128, 128], P('grp'), parts along dimension 0, may hold values from -2.1 to 2.1
- propagator_phase: float32 [128, 128], replicated, may hold values from -3.140625 to 3.140625
- measured: float32 [256, 128, 128], P(('grp', 'row')), parts along dimension 0, may hold values from 0.25 to 4
- offsets: int32 [256, 2], P(('grp', 'row')), parts along dimension 0, may hold values from 0 to 1920, as said below
- counts: int32 [32], P(('grp', 'row')), parts along dimension 0, may hold values from 1 to 8, 72 in all
Outputs:
- object_grad: float32 [2, 2, 2048, 2048], P(None, None, ('grp', 'row')), parts along dimension 2
- probe_step: float32 [8, 2, 128, 128], P('grp'), parts along dimension 0
There are 2 independent parts, one for each index of `grp`. A program takes and returns all parts, laid end to end along the dimension named above; an argument that names none is the same for every part. Nothing has to cross between parts.
Inputs may be any that keep to these rules, and one draw needn't show every extreme that they name: The slots of device d (slots d * 8 to d * 8 + 7) have row offsets d * 64 to d * 64 + 63 and column offsets 0 to 1920. `counts`: counts sum to 72; some device holds 8.
All inputs are finite; a program needn't handle non-finite values.
Results may differ from a plain program's by a relative error of at most 0.0003.
Values sent between devices are 32-bit elements; how exact they have to be, the bound alone decides.
No kernel may reach another device: no remote copies, remote signals or barrier semaphores. Data moves between devices by JAX's collectives and lax.ppermute only.
A program may use at most 64 MiB of HBM per device.

v0:
```python
import functools

import jax
import jax.numpy as jnp
import numpy as np
from jax import lax
from jax.experimental import pallas as pl
from jax.experimental.pallas import tpu as pltpu
from jax.sharding import PartitionSpec as P

CHUNKS = (2, 4, 2)
BATCH = 2
VMEM_LIMIT = 48 * 1024 * 1024
F32 = jnp.float32
BF16 = jnp.bfloat16


def shifted(array, axis, by):
    peers = lax.axis_size(axis)
    return lax.ppermute(array, axis, [(i, (i + by) % peers) for i in range(peers)])


def fourier_tables(pixels):
    indices = np.arange(pixels)
    angles = 2.0 * np.pi * (indices[:, None] * indices[None, :] % pixels) / pixels
    re = np.cos(angles) / np.sqrt(pixels)
    im = -np.sin(angles) / np.sqrt(pixels)
    left = np.block([[re, -im], [im, re]]).astype(np.float32)
    high = left.astype(BF16)
    low = (left - high.astype(np.float32)).astype(BF16)
    return np.stack([high, low, high.T, low.T])


def pieces(array):
    high = array.astype(BF16)
    return high, (array - high.astype(F32)).astype(BF16)


def transform(tables, conj, waves):
    at_left, at_right = (2, 0) if conj else (0, 2)
    left = jnp.concatenate([tables[at_left], tables[at_left + 1], tables[at_left]], axis=1)
    right = jnp.concatenate([tables[at_right], tables[at_right], tables[at_right + 1]], axis=0)
    stacked = jnp.concatenate([jnp.concatenate(wave, axis=0) for wave in waves], axis=1)
    high, low = pieces(stacked)
    half = jnp.dot(left, jnp.concatenate([high, high, low], axis=0), preferred_element_type=F32)
    pixels = half.shape[0] // 2
    places = [i * pixels for i in range(len(waves))]
    turned = jnp.concatenate(
        [
            jnp.concatenate([half[:pixels, at : at + pixels], half[pixels:, at : at + pixels]], axis=1)
            for at in places
        ],
        axis=0,
    )
    high, low = pieces(turned)
    whole = jnp.dot(jnp.concatenate([high, low, high], axis=1), right, preferred_element_type=F32)
    return [(whole[at : at + pixels, :pixels], whole[at : at + pixels, pixels:]) for at in places]


def times(one, two):
    return one[0] * two[0] - one[1] * two[1], one[0] * two[1] + one[1] * two[0]


def conj_times(one, two):
    return one[0] * two[0] + one[1] * two[1], one[0] * two[1] - one[1] * two[0]


def place(column, columns, pixels):
    base = jnp.minimum(column // pixels * pixels, columns - 2 * pixels)
    return pl.multiple_of(base, pixels), column - base


def cut(tile, column, pixels):
    base, shift = place(column, tile.shape[-1], pixels)
    rows = tile.shape[1]
    wide = tile[:, :, pl.ds(base, 2 * pixels)].reshape(-1, 2 * pixels)
    turned = pltpu.roll(wide, 2 * pixels - shift, 1)
    return turned[:, :pixels].reshape(-1, rows, pixels)


def is_even(offsets, rows):
    return lax.rem(offsets[0, 0] // rows, 2) == 0


def cut_kernel(pixels, chunks, own, far, counts, tile, measured, *outs):
    planes, rows, _ = tile.shape
    even = is_even(own, rows)
    for (first, size), near, cross in zip(chunks, outs[::2], outs[1::2]):
        for at in range(size):
            slot = first + at
            near[at, :planes] = cut(tile, jnp.where(even, own[slot, 1], far[slot, 1]), pixels)
            cross[at, :planes] = cut(tile, jnp.where(even, far[slot, 1], own[slot, 1]), pixels)
            live = jnp.where(slot < counts[0], 1.0, 0.0).astype(F32)
            target = (measured[slot] * live).reshape(-1, rows, pixels)
            near[at, planes:] = target
            cross[at, planes:] = target


def add_kernel(pixels, groups, own, middle, far, *refs):
    parts, before, out = refs[: len(groups)], refs[len(groups) : -1], refs[-1]
    rows = out.shape[1]
    even = is_even(own, rows)
    out[...] = before[0][...] if before else jnp.zeros_like(out)
    lane = lax.broadcasted_iota(jnp.int32, (1, 1, pixels), 2)
    for (kind, first), strips in zip(groups, parts):

        def add(at, carry, kind=kind, first=first, strips=strips):
            slot = first + at
            if kind == "mid":
                column = middle[slot, 1]
            elif kind == "near":
                column = jnp.where(even, own[slot, 1], far[slot, 1])
            else:
                column = jnp.where(even, far[slot, 1], own[slot, 1])
            base, shift = place(column, out.shape[-1], pixels)
            part = strips[at]
            turned = pltpu.roll(part.reshape(-1, pixels), lax.rem(shift, pixels), 1).reshape(part.shape)
            out[:, :, pl.ds(base, pixels)] += jnp.where(lane >= shift, turned, 0.0)
            out[:, :, pl.ds(pl.multiple_of(base + pixels, pixels), pixels)] += jnp.where(
                lane < shift, turned, 0.0
            )
            return carry

        lax.fori_loop(0, strips.shape[0], add, 0)


def slot_kernel(
    first, offsets, tile, near, cross, probe, prop, tables, so_far,
    out_near, out_mid, out_cross, total, *refs,
):
    shares, (window, patch, grads, exit_wave, far) = refs[:-5], refs[-5:]
    size = near.shape[0]
    modes, _, pixels, _ = probe.shape
    planes, rows, _ = tile.shape
    even = jnp.logical_not(is_even(offsets, rows))
    total[...] = so_far[...]
    held = [(s, m) for s in range(BATCH) for m in range(modes)]

    def is_live(at):
        return jnp.max(jnp.where(even, cross[at, planes, :8], near[at, planes, :8])) > 0.0

    def leave(slots):
        for at in slots:
            for out in (out_near, out_mid, out_cross):
                out[at] = jnp.zeros(out.shape[1:], F32)

    def visit(slots):
        starts = [lax.rem(offsets[first + at, 0], rows) for at in slots]
        live = [jnp.where(is_live(at), 1.0, 0.0).astype(F32) for at in slots]
        for s, at in enumerate(slots):
            window[:, :rows] = jnp.where(even, cross[at, :planes], near[at, :planes])
            window[:, rows : 2 * rows] = cut(tile, offsets[first + at, 1], pixels)
            window[:, 2 * rows :] = jnp.where(even, near[at, :planes], cross[at, :planes])
            patch[s] = window[:, pl.ds(starts[s], pixels), :]
            total[2 * modes] += live[s] * (patch[s, 0] * patch[s, 0] + patch[s, 1] * patch[s, 1])
        waves = [times((probe[m, 0], probe[m, 1]), (patch[s, 0], patch[s, 1])) for s, m in held]
        waves = transform(tables, False, waves)
        waves = [times((prop[0], prop[1]), wave) for wave in waves]
        waves = transform(tables, True, waves)
        for (s, m), wave in zip(held, waves):
            exit_wave[s, m, 0], exit_wave[s, m, 1] = wave
        waves = [times(wave, (patch[s, 2], patch[s, 3])) for (s, m), wave in zip(held, waves)]
        waves = transform(tables, False, waves)
        intensity = [jnp.zeros((pixels, pixels), F32)] * BATCH
        for (s, m), wave in zip(held, waves):
            far[s, m, 0], far[s, m, 1] = wave
            intensity[s] = intensity[s] + wave[0] * wave[0] + wave[1] * wave[1]
        target = [
            jnp.where(even, cross[at, planes:], near[at, planes:]).reshape(pixels, pixels) for at in slots
        ]
        misfit = [2.0 * live[s] * (intensity[s] - target[s]) for s in range(BATCH)]
        waves = [(misfit[s] * far[s, m, 0], misfit[s] * far[s, m, 1]) for s, m in held]
        waves = transform(tables, True, waves)
        grads[...] = jnp.zeros_like(grads)
        for (s, m), wave in zip(held, waves):
            re, im = conj_times((exit_wave[s, m, 0], exit_wave[s, m, 1]), wave)
            grads[s, 2] += re
            grads[s, 3] += im
        waves = [conj_times((patch[s, 2], patch[s, 3]), wave) for (s, m), wave in zip(held, waves)]
        waves = transform(tables, False, waves)
        waves = [conj_times((prop[0], prop[1]), wave) for wave in waves]
        waves = transform(tables, True, waves)
        for (s, m), wave in zip(held, waves):
            re, im = conj_times((patch[s, 0], patch[s, 1]), wave)
            total[2 * m] += re
            total[2 * m + 1] += im
            re, im = conj_times((probe[m, 0], probe[m, 1]), wave)
            grads[s, 0] += re
            grads[s, 1] += im
        for s, at in enumerate(slots):
            window[...] = jnp.zeros_like(window)
            window[:, pl.ds(starts[s], pixels), :] = grads[s]
            out_near[at] = jnp.where(even, window[:, 2 * rows :], window[:, :rows])
            out_mid[at] = window[:, rows : 2 * rows]
            out_cross[at] = jnp.where(even, window[:, :rows], window[:, 2 * rows :])

    def step(index, carry):
        slots = [index * BATCH + s for s in range(BATCH)]
        some = is_live(slots[0])
        pl.when(some)(lambda: visit(slots))
        pl.when(jnp.logical_not(some))(lambda: leave(slots))
        return carry

    lax.fori_loop(0, size // BATCH, step, 0)

    if shares:
        own, other = shares
        chips, _, share, _ = own.shape
        core = jnp.where(even, 0, 1)
        for chip in range(chips):
            for plane in range(2 * modes + 1):
                own[chip, plane] = total[plane, pl.ds((2 * chip + core) * share, share)]
                other[chip, plane] = total[plane, pl.ds((2 * chip + 1 - core) * share, share)]


def step_kernel(parts, out):
    summed = parts[0]
    for at in range(1, parts.shape[0]):
        summed = summed + parts[at]
    step = summed[:-1] / (summed[-1:] + 1.0)
    for at in range(out.shape[0]):
        out[at] = step


def order_kernel(rows, offsets, own, other, out):
    chips, _, share, _ = own.shape
    core = jnp.where(is_even(offsets, rows), 0, 1)
    for chip in range(chips):
        out[:, pl.ds((2 * chip + core) * share, share)] = own[chip]
        out[:, pl.ds((2 * chip + 1 - core) * share, share)] = other[chip]


def in_smem():
    return pl.BlockSpec(memory_space=pltpu.SMEM)


def in_vmem():
    return pl.BlockSpec(memory_space=pltpu.VMEM)


def local(object_slices, probe_modes, propagator_phase, measured, offsets, counts):
    slices, _, tile_rows, columns = object_slices.shape
    modes, _, pixels, _ = probe_modes.shape
    planes = 2 * slices
    peers = lax.axis_size("row")
    params = pltpu.CompilerParams(vmem_limit_bytes=VMEM_LIMIT)
    tile = object_slices.reshape(planes, tile_rows, columns)
    starts = [sum(CHUNKS[:i]) for i in range(len(CHUNKS))]

    pair = [(i, i ^ 1) for i in range(peers)]
    other_pair = [(i, (i - 1) % peers if i % 2 == 0 else (i + 1) % peers) for i in range(peers)]
    far = shifted(offsets, "row", 2)
    middle = shifted(offsets, "row", 1)

    def strips(chunks):
        shapes = []
        for _, size in chunks:
            message = (size, planes + pixels // tile_rows, tile_rows, pixels)
            shapes += [jax.ShapeDtypeStruct(message, F32)] * 2
        outs = pl.pallas_call(
            functools.partial(cut_kernel, pixels, chunks),
            out_shape=shapes,
            in_specs=[in_smem()] * 3 + [in_vmem()] * 2,
            out_specs=[in_vmem()] * len(shapes),
            compiler_params=params,
            cost_estimate=pl.CostEstimate(flops=0, bytes_accessed=4 << 20, transcendentals=0),
        )(offsets, far, counts, tile, measured)
        return list(zip(outs[::2], outs[1::2]))

    chunks = list(zip(starts, CHUNKS))
    near, cross = [], []
    for to_near, to_cross in strips(chunks[:1]) + strips(chunks[1:]):
        if near:
            to_near, to_cross, _, _ = lax.optimization_barrier((to_near, to_cross, near[-1], cross[-1]))
        cross.append(lax.ppermute(to_cross, "row", other_pair))
        near.append(lax.ppermute(to_near, "row", pair))
    prop = jnp.stack([jnp.cos(propagator_phase), jnp.sin(propagator_phase)])
    tables = jnp.asarray(fourier_tables(pixels))

    share = pixels // peers
    total = jnp.zeros((2 * modes + 1, pixels, pixels), F32)
    mid, back_near, back_cross = [], [], []
    for index, (first, size) in enumerate(zip(starts, CHUNKS)):
        if index >= 2:
            total, back_near[index - 2], back_cross[index - 2] = lax.optimization_barrier(
                (total, back_near[index - 2], back_cross[index - 2])
            )
        strip = jax.ShapeDtypeStruct((size, planes, tile_rows, pixels), F32)
        part = jax.ShapeDtypeStruct((peers // 2, 2 * modes + 1, share, pixels), F32)
        shares = [part, part] if index == len(CHUNKS) - 1 else []
        field = pltpu.VMEM((BATCH, planes, pixels, pixels), F32)
        kept = pltpu.VMEM((BATCH, modes, 2, pixels, pixels), F32)
        to_near, to_mid, to_cross, total, *shares = pl.pallas_call(
            functools.partial(slot_kernel, first),
            out_shape=[strip, strip, strip, jax.ShapeDtypeStruct(total.shape, F32)] + shares,
            in_specs=[in_smem()] + [in_vmem()] * 7,
            out_specs=[in_vmem()] * (4 + len(shares)),
            scratch_shapes=[pltpu.VMEM((planes, 3 * tile_rows, pixels), F32), field, field, kept, kept],
            compiler_params=params,
            cost_estimate=pl.CostEstimate(
                flops=size * 6 * modes * 3 * 16 * pixels**3, bytes_accessed=8 << 20, transcendentals=0
            ),
        )(middle, tile, near[index], cross[index], probe_modes, prop, tables, total)
        mid.append(to_mid)
        back_near.append(lax.ppermute(to_near, "row", pair))
        back_cross.append(lax.ppermute(to_cross, "row", other_pair))

    def added(groups, strips, *before):
        return pl.pallas_call(
            functools.partial(add_kernel, pixels, groups),
            out_shape=jax.ShapeDtypeStruct(tile.shape, F32),
            in_specs=[in_smem()] * 3 + [in_vmem()] * (len(strips) + len(before)),
            out_specs=in_vmem(),
            compiler_params=params,
            input_output_aliases={3 + len(strips): 0} if before else {},
            cost_estimate=pl.CostEstimate(flops=0, bytes_accessed=5 << 20, transcendentals=0),
        )(offsets, middle, far, *strips, *before)

    cores = [list(range(core, peers, 2)) for core in range(2)]
    own, other = shares
    both = own + lax.ppermute(other, "row", pair)
    early = added(
        [("mid", first) for first in starts] + [(kind, first) for first in starts[:-1] for kind in ("near", "cross")],
        mid + [part for parts in zip(back_near[:-1], back_cross[:-1]) for part in parts],
    )
    both, early, last_near, last_cross = lax.optimization_barrier(
        (both, early, back_near[-1], back_cross[-1])
    )
    parts = lax.all_to_all(both, "row", 0, 0, axis_index_groups=cores)
    spread = pl.pallas_call(
        step_kernel,
        out_shape=jax.ShapeDtypeStruct((peers // 2, 2 * modes, share, pixels), F32),
        in_specs=[in_vmem()],
        out_specs=in_vmem(),
        compiler_params=params,
    )(parts)
    gathered = lax.all_to_all(spread, "row", 0, 0, axis_index_groups=cores)

    object_grad = added([("near", starts[-1]), ("cross", starts[-1])], [last_near, last_cross], early)
    object_grad = object_grad.reshape(object_slices.shape)

    probe_step = pl.pallas_call(
        functools.partial(order_kernel, tile_rows),
        out_shape=jax.ShapeDtypeStruct((2 * modes, pixels, pixels), F32),
        in_specs=[in_smem()] + [in_vmem()] * 2,
        out_specs=in_vmem(),
        compiler_params=params,
    )(offsets, gathered, lax.ppermute(gathered, "row", pair)).reshape(probe_modes.shape)
    return (object_grad, probe_step)


def solution(mesh):
    in_specs = (
        P(None, None, ("grp", "row"), None),
        P("grp", None, None, None),
        P(),
        P(("grp", "row"), None, None),
        P(("grp", "row"), None),
        P(("grp", "row")),
    )
    out_specs = (P(None, None, ("grp", "row"), None), P("grp", None, None, None))
    return jax.shard_map(local, mesh=mesh, in_specs=in_specs, out_specs=out_specs, check_vma=False)
```

profile of v0, /device:TPU:1, one launch (start us, length us, event | category | flops | bytes accessed | tf_op | source)
XLA Modules:
  0.0 121.7 jit_solution(8711515217521188431)
XLA Ops:
  0.6 0.8 copy.15.own.offsets
  1.4 2.1 %collective-permute-start.1 = (s32[8,2]{1,0:T(8,128)S(1)}, s32[8,2]{1,0:T(8,128)S(1)}, u32[]{:S(2)}, u32[]{:S(2)}) collective-permute-start(s32[8,2]{1,0:T(8,128)S(1)} %copy.15.own.offsets), channel_id=1, source_target_pairs={{0,2},{1,3},{2,4},{3,5},{4,6},{5,7},{6,8},{7,9},{8,10},{9,11},{10,... | collective-permute-start | bytes 200 | tf_op jit(solution)/shard_map/ppermute | solution.py:20
  4.1 3.4 %collective-permute-done.1.far = s32[8,2]{1,0:T(8,128)S(1)} collective-permute-done((s32[8,2]{1,0:T(8,128)S(1)}, s32[8,2]{1,0:T(8,128)S(1)}, u32[]{:S(2)}, u32[]{:S(2)}) %collective-permute-start.1) | collective-permute-done | bytes 96 | tf_op jit(solution)/shard_map/ppermute | solution.py:20
  7.5 1.6 %copy-done = f32[2,2,64,2048]{3,2,1,0:T(8,128)S(1)} copy-done((f32[2,2,64,2048]{3,2,1,0:T(8,128)S(1)}, f32[2,2,64,2048]{3,2,1,0:T(8,128)}, u32[]{:S(2)}) %copy-start) | copy-done | bytes 2097176
  9.1 1.0 copy-done.2
  10.1 1.0 shard_map.87
  11.1 0.0 copy-start.1
  11.2 0.0 copy-start.3
  11.2 0.0 copy-start.4
  11.2 1.6 %collective-permute-start.2 = (f32[2,6,64,128]{3,2,1,0:T(8,128)S(1)}, f32[2,6,64,128]{3,2,1,0:T(8,128)S(1)}, u32[]{:S(2)}, u32[]{:S(2)}) collective-permute-start(f32[2,6,64,128]{3,2,1,0:T(8,128)S(1)} %get-tuple-element.36), channel_id=1, source_target_pairs={{0,1},{1,0},{2,3},{3,2},{4,5},{5,4},{6,7},{7,6},{8,9},{9,8},{10,11... | collective-permute-start | bytes 1179656 | tf_op jit(solution)/shard_map/ppermute | solution.py:276
  12.8 0.0 collective-permute-start.3
  12.8 1.7 %collective-permute-start = (s32[8,2]{1,0:T(8,128)S(1)}, s32[8,2]{1,0:T(8,128)S(1)}, u32[]{:S(2)}, u32[]{:S(2)}) collective-permute-start(s32[8,2]{1,0:T(8,128)S(1)} %copy.15.own.offsets), channel_id=1, source_target_pairs={{0,1},{1,2},{2,3},{3,4},{4,5},{5,6},{6,7},{7,8},{8,9},{9,10},{10,1... | collective-permute-start | bytes 200 | tf_op jit(solution)/shard_map/ppermute | solution.py:20
  14.5 1.6 %shard_map.86 = (f32[4,6,64,128]{3,2,1,0:T(8,128)S(1)}, f32[4,6,64,128]{3,2,1,0:T(8,128)S(1)}, f32[2,6,64,128]{3,2,1,0:T(8,128)S(1)}, f32[2,6,64,128]{3,2,1,0:T(8,128)S(1)}) custom-call(s32[8,2]{1,0:T(8,128)S(1)} %copy.15.own.offsets, s32[8,2]{1,0:T(8,128)S(1)} %collective-permute-done.1.far, s32[1]{0:T(128)S(6)} %copy.18.counts, ...), custom_call_target="tpu_custom_call" | custom-call | bytes 4194304 | tf_op jit(solution)/shard_map/pallas_call | solution.py:260
  16.1 0.0 collective-permute-done.2.near
  16.1 8.1 %collective-permute-done.3.cross = f32[2,6,64,128]{3,2,1,0:T(8,128)S(1)} collective-permute-done((f32[2,6,64,128]{3,2,1,0:T(8,128)S(1)}, f32[2,6,64,128]{3,2,1,0:T(8,128)S(1)}, u32[]{:S(2)}, u32[]{:S(2)}) %collective-permute-start.3) | collective-permute-done | bytes 393248 | tf_op jit(solution)/shard_map/ppermute | solution.py:275
  24.3 0.0 collective-permute-start.4
  24.3 0.0 collective-permute-start.5
  24.3 0.2 cosine_bitcast_fusion
  24.5 0.0 collective-permute-done.offsets.middle
  24.6 10.1 %shard_map.88 = (f32[2,4,64,128]{3,2,1,0:T(8,128)S(1)}, f32[2,4,64,128]{3,2,1,0:T(8,128)S(1)}, f32[2,4,64,128]{3,2,1,0:T(8,128)S(1)}, f32[9,128,128]{2,1,0:T(8,128)S(1)}) custom-call(s32[8,2]{1,0:T(8,128)S(1)} %collective-permute-done.offsets.middle, f32[4,64,2048]{2,1,0:T(8,128)S(1)} %bitcast.11, f32[2,6,64,128]{3,2,1,0:T(8,128)S(1)} %collective-permute-done.2.near, ...), custom_call_target="tpu_custom_call" | custom-call | flops 4831838208 | bytes 8388608 | tf_op jit(solution)/shard_map/pallas_call | solution.py:293
  34.7 2.2 %collective-permute-start.8 = (f32[2,4,64,128]{3,2,1,0:T(8,128)S(1)}, f32[2,4,64,128]{3,2,1,0:T(8,128)S(1)}, u32[]{:S(2)}, u32[]{:S(2)}) collective-permute-start(f32[2,4,64,128]{3,2,1,0:T(8,128)S(1)} %get-tuple-element.44), channel_id=1, source_target_pairs={{0,1},{1,0},{2,3},{3,2},{4,5},{5,4},{6,7},{7,6},{8,9},{9,8},{10,11... | collective-permute-start | bytes 786440 | tf_op jit(solution)/shard_map/ppermute | solution.py:305
  36.9 0.0 collective-permute-start.9
  36.9 0.0 collective-permute-done.4.near
  36.9 10.0 %collective-permute-done.5.cross = f32[4,6,64,128]{3,2,1,0:T(8,128)S(1)} collective-permute-done((f32[4,6,64,128]{3,2,1,0:T(8,128)S(1)}, f32[4,6,64,128]{3,2,1,0:T(8,128)S(1)}, u32[]{:S(2)}, u32[]{:S(2)}) %collective-permute-start.5) | collective-permute-done | bytes 786464 | tf_op jit(solution)/shard_map/ppermute | solution.py:275
  46.9 0.0 collective-permute-start.6
  46.9 0.0 collective-permute-start.7
  46.9 20.1 %shard_map.89 = (f32[4,4,64,128]{3,2,1,0:T(8,128)S(1)}, f32[4,4,64,128]{3,2,1,0:T(8,128)S(1)}, f32[4,4,64,128]{3,2,1,0:T(8,128)S(1)}, f32[9,128,128]{2,1,0:T(8,128)S(1)}) custom-call(s32[8,2]{1,0:T(8,128)S(1)} %collective-permute-done.offsets.middle, f32[4,64,2048]{2,1,0:T(8,128)} %bitcast.7, f32[4,6,64,128]{3,2,1,0:T(8,128)S(1)} %collective-permute-done.4.near, ...), custom_call_target="tpu_custom_call" | custom-call | flops 9663676416 | bytes 8388608 | tf_op jit(solution)/shard_map/pallas_call | solution.py:293
  67.0 0.0 collective-permute-done.8.refs_3_
  67.0 0.0 collective-permute-done.9.refs_4_
  67.1 2.2 %collective-permute-start.11 = (f32[4,4,64,128]{3,2,1,0:T(8,128)S(1)}, f32[4,4,64,128]{3,2,1,0:T(8,128)S(1)}, u32[]{:S(2)}, u32[]{:S(2)}) collective-permute-start(f32[4,4,64,128]{3,2,1,0:T(8,128)S(1)} %get-tuple-element.54), channel_id=1, source_target_pairs={{0,1},{1,0},{2,3},{3,2},{4,5},{5,4},{6,7},{7,6},{8,9},{9,8},{10,11... | collective-permute-start | bytes 1572872 | tf_op jit(solution)/shard_map/ppermute | solution.py:305
  69.3 0.0 collective-permute-start.12
  69.3 0.0 collective-permute-done.6.near
  69.3 0.0 collective-permute-done.7.cross
  69.3 2.9 %shard_map.90 = (f32[2,4,64,128]{3,2,1,0:T(8,128)S(1)}, f32[2,4,64,128]{3,2,1,0:T(8,128)S(1)}, f32[2,4,64,128]{3,2,1,0:T(8,128)S(1)}, f32[9,128,128]{2,1,0:T(8,1...) custom-call(s32[8,2]{1,0:T(8,128)S(1)} %collective-permute-done.offsets.middle, f32[4,64,2048]{2,1,0:T(8,128)} %bitcast.8, ...), custom_call_target="tpu_custom_call" | custom-call | flops 4831838208 | bytes 8388608 | tf_op jit(solution)/shard_map/pallas_call | solution.py:293
  72.2 1.5 %collective-permute-start.10 = (f32[8,9,8,128]{3,2,1,0:T(8,128)S(1)}, f32[8,9,8,128]{3,2,1,0:T(8,128)S(1)}, u32[]{:S(2)}, u32[]{:S(2)}) collective-permute-start(f32[8,9,8,128]{3,2,1,0:T(8,128)S(1)} %get-tuple-element.48), channel_id=1, source_target_pairs={{0,1},{1,0},{2,3},{3,2},{4,5},{5,4},{6,7},{7,6},{8,9},{9,8},{10,11... | collective-permute-start | bytes 884744 | tf_op jit(solution)/shard_map/ppermute | solution.py:321
  73.7 0.0 collective-permute-start.13
  73.7 9.8 %collective-permute-start.14 = (f32[2,4,64,128]{3,2,1,0:T(8,128)S(1)}, f32[2,4,64,128]{3,2,1,0:T(8,128)S(1)}, u32[]{:S(2)}, u32[]{:S(2)}) collective-permute-start(f32[2,4,64,128]{3,2,1,0:T(8,128)S(1)} %get-tuple-element.57), channel_id=1, source_target_pairs={{0,15},{1,2},{2,1},{3,4},{4,3},{5,6},{6,5},{7,8},{8,7},{9,10},{10,... | collective-permute-start | bytes 786440 | tf_op jit(solution)/shard_map/ppermute | solution.py:306
  83.5 0.0 collective-permute-done.11.refs_5_
  83.5 0.0 collective-permute-done.12.refs_6_
  83.5 5.0 %shard_map.91.refs_2_ = f32[4,64,2048]{2,1,0:T(8,128)} custom-call(s32[8,2]{1,0:T(8,128)S(1)} %copy.15.own.offsets, s32[8,2]{1,0:T(8,128)S(1)} %collective-permute-done.offsets.middle, s32[8,2]{1,0:T(8,128)S(1)} %collective-permute-done.1.far, f32[2,4,64,128]{3,2,1,0:T(8,128)S(1)} %get-tuple-element.49.refs_0_, ...), custom_call_target="tpu_custom_call" | custom-call | bytes 5242880 | tf_op jit(solution)/shard_map/pallas_call | solution.py:309
  88.5 0.0 collective-permute-done.10
  88.5 0.0 collective-permute-done.13.refs_0_
  88.5 1.1 collective-permute-done.14.refs_1_
  89.6 14.2 %all_to_all.10.parts = f32[8,9,8,128]{3,2,1,0:T(8,128)S(1)} all-to-all(f32[8,9,8,128]{3,2,1,0:T(8,128)S(1)} %add.3), channel_id=1, replica_groups={{0,2,4,6,8,10,12,14},{1,3,5,7,9,11,13,15},{16,18,20,22,24,26,28,30},{17..., dimensions={0} | all-to-all | bytes 589824 | tf_op jit(solution)/shard_map/all_to_all | solution.py:329
  103.9 10.1 %all_to_all.11.own = f32[8,8,8,128]{3,2,1,0:T(8,128)S(1)} all-to-all(f32[8,8,8,128]{3,2,1,0:T(8,128)S(1)} %shard_map.93), channel_id=1, replica_groups={{0,2,4,6,8,10,12,14},{1,3,5,7,9,11,13,15},{16,18,20,22,24,26,28,30},{17..., dimensions={0} | all-to-all | bytes 524288 | tf_op jit(solution)/shard_map/all_to_all | solution.py:337
  114.1 2.5 %collective-permute-start.15 = (f32[8,8,8,128]{3,2,1,0:T(8,128)S(1)}, f32[8,8,8,128]{3,2,1,0:T(8,128)S(1)}, u32[]{:S(2)}, u32[]{:S(2)}) collective-permute-start(f32[8,8,8,128]{3,2,1,0:T(8,128)S(1)} %all_to_all.11.own), channel_id=1, source_target_pairs={{0,1},{1,0},{2,3},{3,2},{4,5},{5,4},{6,7},{7,6},{8,9},{9,8},{10,11... | collective-permute-start | bytes 786440 | tf_op jit(solution)/shard_map/ppermute | solution.py:348
  116.6 3.6 %shard_map.92 = f32[4,64,2048]{2,1,0:T(8,128)} custom-call(s32[8,2]{1,0:T(8,128)S(1)} %copy.15.own.offsets, s32[8,2]{1,0:T(8,128)S(1)} %collective-permute-done.offsets.middle, s32[8,2]{1,0:T(8,128)S(1)} %collective-permute-done.1.far, f32[2,4,64,128]{3,2,1,0:T(8,128)S(1)} %collective-permute-done.13.refs_0_, ...), custom_call_target="tpu_custom_call", output_to_operand_aliasing={{}: (5, {})} | custom-call | bytes 5242880 | tf_op jit(solution)/shard_map/pallas_call | solution.py:309
  120.2 1.5 %shard_map.94 = f32[8,128,128]{2,1,0:T(8,128)} custom-call(s32[8,2]{1,0:T(8,128)S(1)} %copy.15.own.offsets, f32[8,8,8,128]{3,2,1,0:T(8,128)S(1)} %all_to_all.11.own, f32[8,8,8,128]{3,2,1,0:T(8,128)S(1)} %collective-permute-done.15.other), custom_call_target="tpu_custom_call" | custom-call | tf_op jit(solution)/shard_map/pallas_call | solution.py:342
  (12 shorter events, 0.1 us)
Async XLA Ops:
  1.4 6.1 %collective-permute-start.1 = (s32[8,2]{1,0:T(8,128)S(1)}, s32[8,2]{1,0:T(8,128)S(1)}, u32[]{:S(2)}, u32[]{:S(2)}) collective-permute-start(s32[8,2]{1,0:T(8,128)S(1)} %copy.15.own.offsets), channel_id=1, source_target_pairs={{0,2},{1,3},{2,4},{3,5},{4,6},{5,7},{6,8},{7,9},{8,10},{9,11},{10,... | collective-permute-start | bytes 200 | tf_op jit(solution)/shard_map/ppermute | solution.py:20
  7.5 1.6 %copy-start = (f32[2,2,64,2048]{3,2,1,0:T(8,128)S(1)}, f32[2,2,64,2048]{3,2,1,0:T(8,128)}, u32[]{:S(2)}) copy-start(f32[2,2,64,2048]{3,2,1,0:T(8,128)} %param.7) | copy-start | bytes 6291460
  9.1 1.0 copy-start.2
  10.1 14.1 %copy-start.5 = (f32[128,128]{1,0:T(8,128)S(1)}, f32[128,128]{1,0:T(8,128)}, u32[]{:S(2)}) copy-start(f32[128,128]{1,0:T(8,128)} %param.9) | copy-start | bytes 196612
  11.1 13.4 %copy-start.1 = (f32[2,2,64,2048]{3,2,1,0:T(8,128)S(1)}, f32[2,2,64,2048]{3,2,1,0:T(8,128)}, u32[]{:S(2)}) copy-start(f32[2,2,64,2048]{3,2,1,0:T(8,128)} %param.7) | copy-start | bytes 6291460
  11.2 13.4 %copy-start.3 = (f32[4,2,128,128]{3,2,1,0:T(8,128)S(1)}, f32[4,2,128,128]{3,2,1,0:T(8,128)}, u32[]{:S(2)}) copy-start(f32[4,2,128,128]{3,2,1,0:T(8,128)} %probe.5) | copy-start | bytes 1572868
  11.2 13.4 %copy-start.4 = (bf16[4,256,256]{2,1,0:T(8,128)(2,1)S(1)}, bf16[4,256,256]{2,1,0:T(8,128)(2,1)}, u32[]{:S(2)}) copy-start(bf16[4,256,256]{2,1,0:T(8,128)(2,1)} %constant.4.clone.tables) | copy-start | bytes 1572868
  11.2 4.9 %collective-permute-start.2 = (f32[2,6,64,128]{3,2,1,0:T(8,128)S(1)}, f32[2,6,64,128]{3,2,1,0:T(8,128)S(1)}, u32[]{:S(2)}, u32[]{:S(2)}) collective-permute-start(f32[2,6,64,128]{3,2,1,0:T(8,128)S(1)} %get-tuple-element.36), channel_id=1, source_target_pairs={{0,1},{1,0},{2,3},{3,2},{4,5},{5,4},{6,7},{7,6},{8,9},{9,8},{10,11... | collective-permute-start | bytes 1179656 | tf_op jit(solution)/shard_map/ppermute | solution.py:276
  12.8 11.5 %collective-permute-start.3 = (f32[2,6,64,128]{3,2,1,0:T(8,128)S(1)}, f32[2,6,64,128]{3,2,1,0:T(8,128)S(1)}, u32[]{:S(2)}, u32[]{:S(2)}) collective-permute-start(f32[2,6,64,128]{3,2,1,0:T(8,128)S(1)} %get-tuple-element.37), channel_id=1, source_target_pairs={{0,15},{1,2},{2,1},{3,4},{4,3},{5,6},{6,5},{7,8},{8,7},{9,10},{10,... | collective-permute-start | bytes 1179656 | tf_op jit(solution)/shard_map/ppermute | solution.py:275
  12.8 11.7 %collective-permute-start = (s32[8,2]{1,0:T(8,128)S(1)}, s32[8,2]{1,0:T(8,128)S(1)}, u32[]{:S(2)}, u32[]{:S(2)}) collective-permute-start(s32[8,2]{1,0:T(8,128)S(1)} %copy.15.own.offsets), channel_id=1, source_target_pairs={{0,1},{1,2},{2,3},{3,4},{4,5},{5,6},{6,7},{7,8},{8,9},{9,10},{10,1... | collective-permute-start | bytes 200 | tf_op jit(solution)/shard_map/ppermute | solution.py:20
  24.3 12.7 %collective-permute-start.4 = (f32[4,6,64,128]{3,2,1,0:T(8,128)S(1)}, f32[4,6,64,128]{3,2,1,0:T(8,128)S(1)}, u32[]{:S(2)}, u32[]{:S(2)}) collective-permute-start(f32[4,6,64,128]{3,2,1,0:T(8,128)S(1)} %get-tuple-element.38), channel_id=1, source_target_pairs={{0,1},{1,0},{2,3},{3,2},{4,5},{5,4},{6,7},{7,6},{8,9},{9,8},{10,11... | collective-permute-start | bytes 2359304 | tf_op jit(solution)/shard_map/ppermute | solution.py:276
  24.3 22.7 %collective-permute-start.5 = (f32[4,6,64,128]{3,2,1,0:T(8,128)S(1)}, f32[4,6,64,128]{3,2,1,0:T(8,128)S(1)}, u32[]{:S(2)}, u32[]{:S(2)}) collective-permute-start(f32[4,6,64,128]{3,2,1,0:T(8,128)S(1)} %get-tuple-element.39), channel_id=1, source_target_pairs={{0,15},{1,2},{2,1},{3,4},{4,3},{5,6},{6,5},{7,8},{8,7},{9,10},{10,... | collective-permute-start | bytes 2359304 | tf_op jit(solution)/shard_map/ppermute | solution.py:275
  34.7 32.4 %collective-permute-start.8 = (f32[2,4,64,128]{3,2,1,0:T(8,128)S(1)}, f32[2,4,64,128]{3,2,1,0:T(8,128)S(1)}, u32[]{:S(2)}, u32[]{:S(2)}) collective-permute-start(f32[2,4,64,128]{3,2,1,0:T(8,128)S(1)} %get-tuple-element.44), channel_id=1, source_target_pairs={{0,1},{1,0},{2,3},{3,2},{4,5},{5,4},{6,7},{7,6},{8,9},{9,8},{10,11... | collective-permute-start | bytes 786440 | tf_op jit(solution)/shard_map/ppermute | solution.py:305
  36.9 30.1 %collective-permute-start.9 = (f32[2,4,64,128]{3,2,1,0:T(8,128)S(1)}, f32[2,4,64,128]{3,2,1,0:T(8,128)S(1)}, u32[]{:S(2)}, u32[]{:S(2)}) collective-permute-start(f32[2,4,64,128]{3,2,1,0:T(8,128)S(1)} %get-tuple-element.45), channel_id=1, source_target_pairs={{0,15},{1,2},{2,1},{3,4},{4,3},{5,6},{6,5},{7,8},{8,7},{9,10},{10,... | collective-permute-start | bytes 786440 | tf_op jit(solution)/shard_map/ppermute | solution.py:306
  46.9 22.4 %collective-permute-start.6 = (f32[2,6,64,128]{3,2,1,0:T(8,128)S(1)}, f32[2,6,64,128]{3,2,1,0:T(8,128)S(1)}, u32[]{:S(2)}, u32[]{:S(2)}) collective-permute-start(f32[2,6,64,128]{3,2,1,0:T(8,128)S(1)} %get-tuple-element.40), channel_id=1, source_target_pairs={{0,1},{1,0},{2,3},{3,2},{4,5},{5,4},{6,7},{7,6},{8,9},{9,8},{10,11... | collective-permute-start | bytes 1179656 | tf_op jit(solution)/shard_map/ppermute | solution.py:276
  46.9 22.4 %collective-permute-start.7 = (f32[2,6,64,128]{3,2,1,0:T(8,128)S(1)}, f32[2,6,64,128]{3,2,1,0:T(8,128)S(1)}, u32[]{:S(2)}, u32[]{:S(2)}) collective-permute-start(f32[2,6,64,128]{3,2,1,0:T(8,128)S(1)} %get-tuple-element.41), channel_id=1, source_target_pairs={{0,15},{1,2},{2,1},{3,4},{4,3},{5,6},{6,5},{7,8},{8,7},{9,10},{10,... | collective-permute-start | bytes 1179656 | tf_op jit(solution)/shard_map/ppermute | solution.py:275
  67.1 16.5 %collective-permute-start.11 = (f32[4,4,64,128]{3,2,1,0:T(8,128)S(1)}, f32[4,4,64,128]{3,2,1,0:T(8,128)S(1)}, u32[]{:S(2)}, u32[]{:S(2)}) collective-permute-start(f32[4,4,64,128]{3,2,1,0:T(8,128)S(1)} %get-tuple-element.54), channel_id=1, source_target_pairs={{0,1},{1,0},{2,3},{3,2},{4,5},{5,4},{6,7},{7,6},{8,9},{9,8},{10,11... | collective-permute-start | bytes 1572872 | tf_op jit(solution)/shard_map/ppermute | solution.py:305
  69.3 14.2 %collective-permute-start.12 = (f32[4,4,64,128]{3,2,1,0:T(8,128)S(1)}, f32[4,4,64,128]{3,2,1,0:T(8,128)S(1)}, u32[]{:S(2)}, u32[]{:S(2)}) collective-permute-start(f32[4,4,64,128]{3,2,1,0:T(8,128)S(1)} %get-tuple-element.55), channel_id=1, source_target_pairs={{0,15},{1,2},{2,1},{3,4},{4,3},{5,6},{6,5},{7,8},{8,7},{9,10},{10,... | collective-permute-start | bytes 1572872 | tf_op jit(solution)/shard_map/ppermute | solution.py:306
  72.2 16.3 %collective-permute-start.10 = (f32[8,9,8,128]{3,2,1,0:T(8,128)S(1)}, f32[8,9,8,128]{3,2,1,0:T(8,128)S(1)}, u32[]{:S(2)}, u32[]{:S(2)}) collective-permute-start(f32[8,9,8,128]{3,2,1,0:T(8,128)S(1)} %get-tuple-element.48), channel_id=1, source_target_pairs={{0,1},{1,0},{2,3},{3,2},{4,5},{5,4},{6,7},{7,6},{8,9},{9,8},{10,11... | collective-permute-start | bytes 884744 | tf_op jit(solution)/shard_map/ppermute | solution.py:321
  73.7 14.8 %collective-permute-start.13 = (f32[2,4,64,128]{3,2,1,0:T(8,128)S(1)}, f32[2,4,64,128]{3,2,1,0:T(8,128)S(1)}, u32[]{:S(2)}, u32[]{:S(2)}) collective-permute-start(f32[2,4,64,128]{3,2,1,0:T(8,128)S(1)} %get-tuple-element.56), channel_id=1, source_target_pairs={{0,1},{1,0},{2,3},{3,2},{4,5},{5,4},{6,7},{7,6},{8,9},{9,8},{10,11... | collective-permute-start | bytes 786440 | tf_op jit(solution)/shard_map/ppermute | solution.py:305
  73.7 15.9 %collective-permute-start.14 = (f32[2,4,64,128]{3,2,1,0:T(8,128)S(1)}, f32[2,4,64,128]{3,2,1,0:T(8,128)S(1)}, u32[]{:S(2)}, u32[]{:S(2)}) collective-permute-start(f32[2,4,64,128]{3,2,1,0:T(8,128)S(1)} %get-tuple-element.57), channel_id=1, source_target_pairs={{0,15},{1,2},{2,1},{3,4},{4,3},{5,6},{6,5},{7,8},{8,7},{9,10},{10,... | collective-permute-start | bytes 786440 | tf_op jit(solution)/shard_map/ppermute | solution.py:306
  114.1 6.2 %collective-permute-start.15 = (f32[8,8,8,128]{3,2,1,0:T(8,128)S(1)}, f32[8,8,8,128]{3,2,1,0:T(8,128)S(1)}, u32[]{:S(2)}, u32[]{:S(2)}) collective-permute-start(f32[8,8,8,128]{3,2,1,0:T(8,128)S(1)} %all_to_all.11.own), channel_id=1, source_target_pairs={{0,1},{1,0},{2,3},{3,2},{4,5},{5,4},{6,7},{7,6},{8,9},{9,8},{10,11... | collective-permute-start | bytes 786440 | tf_op jit(solution)/shard_map/ppermute | solution.py:348
where the time goes:
time: 122 us
  Pallas kernels  45.7 us (37%)
  blocking collectives  24.4 us (20%)
  starting transfers between devices  23.7 us (19%)
  waiting for transfers between devices  22.6 us (19%)
  local copies, waits for them, and re-layouts  3.69 us (3%)
  between operations  1.46 us (1%)
    pallas_call x3, Pallas kernels, local(): pl.pallas_call(functools.partial(slot_kernel, first), out_shape=[strip, s...  33.1 us
    ppermute x3, waiting for transfers between devices, local(): cross.append(lax.ppermute(to_cross, 'row', other_pair))  18.1 us
    all_to_all x1, blocking collectives, local(): parts = lax.all_to_all(both, 'row', 0, 0, axis_index_groups=cores)  14.2 us
    all_to_all x1, blocking collectives, local(): gathered = lax.all_to_all(spread, 'row', 0, 0, axis_index_groups=cores)  10.1 us
    ppermute x3, starting transfers between devices, local(): back_cross.append(lax.ppermute(to_cross, 'row', other_pair))  9.82 us
    pallas_call x2, Pallas kernels, added(): pl.pallas_call(functools.partial(add_kernel, pixels, groups), out_shape=j...  8.6 us
    ppermute x3, starting transfers between devices, local(): back_near.append(lax.ppermute(to_near, 'row', pair))  4.45 us
    ppermute x2, starting transfers between devices, shifted(): lax.ppermute(array, axis, [(i, (i + by) % peers) for i in range(peers)])  3.81 us
  transfers between devices with their start and end apart: 16, of which 4 were waited for; matrix products, arithmetic and copies ran while one was open for 0% of the time, Pallas kernels for 36%

commit v1 on v0

--- a/solution.py
+++ b/solution.py
@@ -85,26 +85,27 @@
 def cut_kernel(pixels, chunks, own, far, counts, tile, measured, *outs):
     planes, rows, _ = tile.shape
     even = is_even(own, rows)
-    for (first, size), near, cross in zip(chunks, outs[::2], outs[1::2]):
+    for (first, size), near, cross in zip(chunks, outs[::2], outs[1::2], strict=True):
         for at in range(size):
             slot = first + at
-            near[at, :planes] = cut(tile, jnp.where(even, own[slot, 1], far[slot, 1]), pixels)
-            cross[at, :planes] = cut(tile, jnp.where(even, far[slot, 1], own[slot, 1]), pixels)
+            strip = at * (planes + pixels // rows)
+            near[strip : strip + planes] = cut(tile, jnp.where(even, own[slot, 1], far[slot, 1]), pixels)
+            cross[strip : strip + planes] = cut(tile, jnp.where(even, far[slot, 1], own[slot, 1]), pixels)
             live = jnp.where(slot < counts[0], 1.0, 0.0).astype(F32)
             target = (measured[slot] * live).reshape(-1, rows, pixels)
-            near[at, planes:] = target
-            cross[at, planes:] = target
+            near[strip + planes : strip + planes + pixels // rows] = target
+            cross[strip + planes : strip + planes + pixels // rows] = target
 
 
 def add_kernel(pixels, groups, own, middle, far, *refs):
     parts, before, out = refs[: len(groups)], refs[len(groups) : -1], refs[-1]
-    rows = out.shape[1]
+    planes, rows, _ = out.shape
     even = is_even(own, rows)
     out[...] = before[0][...] if before else jnp.zeros_like(out)
     lane = lax.broadcasted_iota(jnp.int32, (1, 1, pixels), 2)
-    for (kind, first), strips in zip(groups, parts):
-
-        def add(at, carry, kind=kind, first=first, strips=strips):
+    for (kind, first, size, unit), strips in zip(groups, parts):
+
+        def add(at, carry, kind=kind, first=first, unit=unit, strips=strips):
             slot = first + at
             if kind == "mid":
                 column = middle[slot, 1]
@@ -113,7 +114,7 @@
             else:
                 column = jnp.where(even, far[slot, 1], own[slot, 1])
             base, shift = place(column, out.shape[-1], pixels)
-            part = strips[at]
+            part = strips[pl.ds(unit + at * planes, planes)]
             turned = pltpu.roll(part.reshape(-1, pixels), lax.rem(shift, pixels), 1).reshape(part.shape)
             out[:, :, pl.ds(base, pixels)] += jnp.where(lane >= shift, turned, 0.0)
             out[:, :, pl.ds(pl.multiple_of(base + pixels, pixels), pixels)] += jnp.where(
@@ -121,36 +122,42 @@
             )
             return carry
 
-        lax.fori_loop(0, strips.shape[0], add, 0)
+        lax.fori_loop(0, size, add, 0)
 
 
 def slot_kernel(
-    first, offsets, tile, near, cross, probe, prop, tables, so_far,
-    out_near, out_mid, out_cross, total, *refs,
+    first, size, ahead, offsets, tile, near, cross, probe, prop, tables, so_far, *refs
 ):
-    shares, (window, patch, grads, exit_wave, far) = refs[:-5], refs[-5:]
-    size = near.shape[0]
+    given, refs = refs[:ahead], refs[ahead:]
+    out_near, out_mid, out_cross, total, *shares = refs[:-5]
+    window, patch, grads, exit_wave, far = refs[-5:]
     modes, _, pixels, _ = probe.shape
     planes, rows, _ = tile.shape
+    each = planes + pixels // rows
+    behind = given[0].shape[0] if given else 0
+    for message, out in zip(given, (out_near, out_cross)):
+        out[:behind] = message[...]
     even = jnp.logical_not(is_even(offsets, rows))
     total[...] = so_far[...]
     held = [(s, m) for s in range(BATCH) for m in range(modes)]
 
     def is_live(at):
-        return jnp.max(jnp.where(even, cross[at, planes, :8], near[at, planes, :8])) > 0.0
+        unit = at * each + planes
+        return jnp.max(jnp.where(even, cross[unit, :8], near[unit, :8])) > 0.0
 
     def leave(slots):
         for at in slots:
-            for out in (out_near, out_mid, out_cross):
-                out[at] = jnp.zeros(out.shape[1:], F32)
+            for out, unit in ((out_near, behind), (out_mid, 0), (out_cross, behind)):
+                out[pl.ds(unit + at * planes, planes)] = jnp.zeros((planes, rows, pixels), F32)
 
     def visit(slots):
         starts = [lax.rem(offsets[first + at, 0], rows) for at in slots]
         live = [jnp.where(is_live(at), 1.0, 0.0).astype(F32) for at in slots]
         for s, at in enumerate(slots):
-            window[:, :rows] = jnp.where(even, cross[at, :planes], near[at, :planes])
+            strip = pl.ds(at * each, planes)
+            window[:, :rows] = jnp.where(even, cross[strip], near[strip])
             window[:, rows : 2 * rows] = cut(tile, offsets[first + at, 1], pixels)
-            window[:, 2 * rows :] = jnp.where(even, near[at, :planes], cross[at, :planes])
+            window[:, 2 * rows :] = jnp.where(even, near[strip], cross[strip])
             patch[s] = window[:, pl.ds(starts[s], pixels), :]
             total[2 * modes] += live[s] * (patch[s, 0] * patch[s, 0] + patch[s, 1] * patch[s, 1])
         waves = [times((probe[m, 0], probe[m, 1]), (patch[s, 0], patch[s, 1])) for s, m in held]
@@ -165,9 +172,8 @@
         for (s, m), wave in zip(held, waves):
             far[s, m, 0], far[s, m, 1] = wave
             intensity[s] = intensity[s] + wave[0] * wave[0] + wave[1] * wave[1]
-        target = [
-            jnp.where(even, cross[at, planes:], near[at, planes:]).reshape(pixels, pixels) for at in slots
-        ]
+        units = [pl.ds(at * each + planes, each - planes) for at in slots]
+        target = [jnp.where(even, cross[unit], near[unit]).reshape(pixels, pixels) for unit in units]
         misfit = [2.0 * live[s] * (intensity[s] - target[s]) for s in range(BATCH)]
         waves = [(misfit[s] * far[s, m, 0], misfit[s] * far[s, m, 1]) for s, m in held]
         waves = transform(tables, True, waves)
@@ -190,9 +196,10 @@
         for s, at in enumerate(slots):
             window[...] = jnp.zeros_like(window)
             window[:, pl.ds(starts[s], pixels), :] = grads[s]
-            out_near[at] = jnp.where(even, window[:, 2 * rows :], window[:, :rows])
-            out_mid[at] = window[:, rows : 2 * rows]
-            out_cross[at] = jnp.where(even, window[:, :rows], window[:, 2 * rows :])
+            strip = pl.ds(behind + at * planes, planes)
+            out_near[strip] = jnp.where(even, window[:, 2 * rows :], window[:, :rows])
+            out_mid[pl.ds(at * planes, planes)] = window[:, rows : 2 * rows]
+            out_cross[strip] = jnp.where(even, window[:, :rows], window[:, 2 * rows :])
 
     def step(index, carry):
         slots = [index * BATCH + s for s in range(BATCH)]
@@ -252,11 +259,13 @@
     far = shifted(offsets, "row", 2)
     middle = shifted(offsets, "row", 1)
 
+    each = planes + pixels // tile_rows
+
+    def units(count):
+        return jax.ShapeDtypeStruct((count, tile_rows, pixels), F32)
+
     def strips(chunks):
-        shapes = []
-        for _, size in chunks:
-            message = (size, planes + pixels // tile_rows, tile_rows, pixels)
-            shapes += [jax.ShapeDtypeStruct(message, F32)] * 2
+        shapes = [units(size * each) for _, size in chunks for _ in range(2)]
         outs = pl.pallas_call(
             functools.partial(cut_kernel, pixels, chunks),
             out_shape=shapes,
@@ -267,43 +276,42 @@
         )(offsets, far, counts, tile, measured)
         return list(zip(outs[::2], outs[1::2]))
 
+    def swapped(to_near, to_cross):
+        return lax.ppermute(to_near, "row", pair), lax.ppermute(to_cross, "row", other_pair)
+
     chunks = list(zip(starts, CHUNKS))
-    near, cross = [], []
-    for to_near, to_cross in strips(chunks[:1]) + strips(chunks[1:]):
-        if near:
-            to_near, to_cross, _, _ = lax.optimization_barrier((to_near, to_cross, near[-1], cross[-1]))
-        cross.append(lax.ppermute(to_cross, "row", other_pair))
-        near.append(lax.ppermute(to_near, "row", pair))
+    waiting = strips(chunks[:1]) + strips(chunks[1:])
+    arrived = [swapped(*message) for message in waiting[:2]]
     prop = jnp.stack([jnp.cos(propagator_phase), jnp.sin(propagator_phase)])
     tables = jnp.asarray(fourier_tables(pixels))
 
     share = pixels // peers
     total = jnp.zeros((2 * modes + 1, pixels, pixels), F32)
-    mid, back_near, back_cross = [], [], []
-    for index, (first, size) in enumerate(zip(starts, CHUNKS)):
-        if index >= 2:
-            total, back_near[index - 2], back_cross[index - 2] = lax.optimization_barrier(
-                (total, back_near[index - 2], back_cross[index - 2])
-            )
-        strip = jax.ShapeDtypeStruct((size, planes, tile_rows, pixels), F32)
+    mid, back = [], []
+    for index, (first, size) in enumerate(chunks):
+        given = waiting[index + 2] if index + 2 < len(chunks) else ()
+        ahead = CHUNKS[index + 2] * each if given else 0
         part = jax.ShapeDtypeStruct((peers // 2, 2 * modes + 1, share, pixels), F32)
         shares = [part, part] if index == len(CHUNKS) - 1 else []
+        message = units(ahead + size * planes)
         field = pltpu.VMEM((BATCH, planes, pixels, pixels), F32)
         kept = pltpu.VMEM((BATCH, modes, 2, pixels, pixels), F32)
         to_near, to_mid, to_cross, total, *shares = pl.pallas_call(
-            functools.partial(slot_kernel, first),
-            out_shape=[strip, strip, strip, jax.ShapeDtypeStruct(total.shape, F32)] + shares,
-            in_specs=[in_smem()] + [in_vmem()] * 7,
+            functools.partial(slot_kernel, first, size, len(given)),
+            out_shape=[message, units(size * planes), message, jax.ShapeDtypeStruct(total.shape, F32)] + shares,
+            in_specs=[in_smem()] + [in_vmem()] * (7 + len(given)),
             out_specs=[in_vmem()] * (4 + len(shares)),
             scratch_shapes=[pltpu.VMEM((planes, 3 * tile_rows, pixels), F32), field, field, kept, kept],
             compiler_params=params,
             cost_estimate=pl.CostEstimate(
                 flops=size * 6 * modes * 3 * 16 * pixels**3, bytes_accessed=8 << 20, transcendentals=0
             ),
-        )(middle, tile, near[index], cross[index], probe_modes, prop, tables, total)
-        mid.append(to_mid)
-        back_near.append(lax.ppermute(to_near, "row", pair))
-        back_cross.append(lax.ppermute(to_cross, "row", other_pair))
+        )(middle, tile, *arrived[index], probe_modes, prop, tables, total, *given)
+        mid.append((("mid", first, size, 0), to_mid))
+        message = swapped(to_near, to_cross)
+        if given:
+            arrived.append(message)
+        back.append([((kind, first, size, ahead), part) for kind, part in zip(("near", "cross"), message)])
 
     def added(groups, strips, *before):
         return pl.pallas_call(
@@ -319,13 +327,9 @@
     cores = [list(range(core, peers, 2)) for core in range(2)]
     own, other = shares
     both = own + lax.ppermute(other, "row", pair)
-    early = added(
-        [("mid", first) for first in starts] + [(kind, first) for first in starts[:-1] for kind in ("near", "cross")],
-        mid + [part for parts in zip(back_near[:-1], back_cross[:-1]) for part in parts],
-    )
-    both, early, last_near, last_cross = lax.optimization_barrier(
-        (both, early, back_near[-1], back_cross[-1])
-    )
+    early = added(*zip(*(mid + [part for parts in back[:-1] for part in parts])))
+    last_groups, last_strips = zip(*back[-1])
+    both, early, last_strips = lax.optimization_barrier((both, early, last_strips))
     parts = lax.all_to_all(both, "row", 0, 0, axis_index_groups=cores)
     spread = pl.pallas_call(
         step_kernel,
@@ -336,7 +340,7 @@
     )(parts)
     gathered = lax.all_to_all(spread, "row", 0, 0, axis_index_groups=cores)
 
-    object_grad = added([("near", starts[-1]), ("cross", starts[-1])], [last_near, last_cross], early)
+    object_grad = added(last_groups, last_strips, early)
     object_grad = object_grad.reshape(object_slices.shape)
 
     probe_step = pl.pallas_call(

time: 122 us -> 120 us (0.984)
  Pallas kernels: 45.7 us -> 28.7 us
  starting transfers between devices: 23.7 us -> 31.1 us
  waiting for transfers between devices: 22.6 us -> 27.3 us
  blocking collectives: 24.4 us -> 26.5 us
    pallas_call x3, Pallas kernels: 33.1 us -> 16 us  [local(): pl.pallas_call(functools.partial(slot_kernel, first, size, len(given)), o...]
    ppermute x2, waiting for transfers between devices: 3.38 us -> 16.7 us  [shifted(): lax.ppermute(array, axis, [(i, (i + by) % peers) for i in range(peers)])]
    ppermute x12 -> x10, waiting for transfers between devices: 19.2 us -> 10.5 us  [the longest x5 10.5 us: swapped(): lax.ppermute(to_cross, 'row', other_pair)]
    ppermute x12 -> x10, starting transfers between devices: 15.9 us -> 22 us  [the longest x5 22 us: swapped(): lax.ppermute(to_near, 'row', pair)]
    all_to_all x1, blocking collectives: 14.2 us -> 16.2 us  [local(): parts = lax.all_to_all(both, 'row', 0, 0, axis_index_groups=cores)]
    ppermute x1, starting transfers between devices: 1.48 us -> 3.26 us  [local(): both = own + lax.ppermute(other, 'row', pair)]
    unnamed x13 -> x11, local copies, waits for them, and re-layouts: 3.41 us -> 3.4 us
  transfers between devices with their start and end apart: 16 -> 14, of which waited for: 4 -> 4; matrix products, arithmetic and copies ran while one was open for 0% -> 0% of each run, Pallas kernels for 36% -> 22%
where the time goes in v1:
time: 120 us; the launch traced here: 119 us
  starting transfers between devices  31.1 us (26%)
  Pallas kernels  28.7 us (24%)
  waiting for transfers between devices  27.3 us (23%)
  blocking collectives  26.5 us (22%)
  local copies, waits for them, and re-layouts  3.68 us (3%)
  between operations  1.44 us (1%)
    ppermute x5, starting transfers between devices, swapped(): lax.ppermute(to_near, 'row', pair)  22 us
    ppermute x2, waiting for transfers between devices, shifted(): lax.ppermute(array, axis, [(i, (i + by) % peers) for i in range(peers)])  16.7 us
    all_to_all x1, blocking collectives, local(): parts = lax.all_to_all(both, 'row', 0, 0, axis_index_groups=cores)  16.2 us
    pallas_call x3, Pallas kernels, local(): pl.pallas_call(functools.partial(slot_kernel, first, size, len(given)), o...  16 us
    ppermute x5, waiting for transfers between devices, swapped(): lax.ppermute(to_cross, 'row', other_pair)  10.5 us
    all_to_all x1, blocking collectives, local(): gathered = lax.all_to_all(spread, 'row', 0, 0, axis_index_groups=cores)  10.3 us
    pallas_call x2, Pallas kernels, added(): pl.pallas_call(functools.partial(add_kernel, pixels, groups), out_shape=j...  8.6 us
    ppermute x2, starting transfers between devices, shifted(): lax.ppermute(array, axis, [(i, (i + by) % peers) for i in range(peers)])  3.81 us
  transfers between devices with their start and end apart: 14, of which 4 were waited for; matrix products, arithmetic and copies ran while one was open for 0% of the time, Pallas kernels for 22%

profile of v1, /device:TPU:1, one launch (start us, length us, event | category | flops | bytes accessed | tf_op | source)
XLA Modules:
  0.0 118.7 jit_solution(17270207055270933945)
XLA Ops:
  0.6 0.8 copy.15.own.offsets
  1.4 2.1 %collective-permute-start.1 = (s32[8,2]{1,0:T(8,128)S(1)}, s32[8,2]{1,0:T(8,128)S(1)}, u32[]{:S(2)}, u32[]{:S(2)}) collective-permute-start(s32[8,2]{1,0:T(8,128)S(1)} %copy.15.own.offsets), channel_id=1, source_target_pairs={{0,2},{1,3},{2,4},{3,5},{4,6},{5,7},{6,8},{7,9},{8,10},{9,11},{10,... | collective-permute-start | bytes 200 | tf_op jit(solution)/shard_map/ppermute | solution.py:20
  4.1 3.4 %collective-permute-done.1.far = s32[8,2]{1,0:T(8,128)S(1)} collective-permute-done((s32[8,2]{1,0:T(8,128)S(1)}, s32[8,2]{1,0:T(8,128)S(1)}, u32[]{:S(2)}, u32[]{:S(2)}) %collective-permute-start.1) | collective-permute-done | bytes 96 | tf_op jit(solution)/shard_map/ppermute | solution.py:20
  7.5 0.0 copy-start
  7.5 1.6 %copy-done = f32[2,2,64,2048]{3,2,1,0:T(8,128)S(1)} copy-done((f32[2,2,64,2048]{3,2,1,0:T(8,128)S(1)}, f32[2,2,64,2048]{3,2,1,0:T(8,128)}, u32[]{:S(2)}) %copy-start) | copy-done | bytes 2097176
  9.1 1.0 copy-done.1
  10.1 1.0 shard_map.86
  11.1 0.0 copy-start.2
  11.2 0.0 copy-start.3
  11.2 1.6 %collective-permute-start.2 = (f32[12,64,128]{2,1,0:T(8,128)S(1)}, f32[12,64,128]{2,1,0:T(8,128)S(1)}, u32[]{:S(2)}, u32[]{:S(2)}) collective-permute-start(f32[12,64,128]{2,1,0:T(8,128)S(1)} %get-tuple-element.25), channel_id=1, source_target_pairs={{0,1},{1,0},{2,3},{3,2},{4,5},{5,4},{6,7},{7,6},{8,9},{9,8},{10,11... | collective-permute-start | bytes 1179656 | tf_op jit(solution)/shard_map/ppermute | solution.py:280
  12.8 0.0 collective-permute-start.3
  12.8 1.7 %collective-permute-start = (s32[8,2]{1,0:T(8,128)S(1)}, s32[8,2]{1,0:T(8,128)S(1)}, u32[]{:S(2)}, u32[]{:S(2)}) collective-permute-start(s32[8,2]{1,0:T(8,128)S(1)} %copy.15.own.offsets), channel_id=1, source_target_pairs={{0,1},{1,2},{2,3},{3,4},{4,5},{5,6},{6,7},{7,8},{8,9},{9,10},{10,1... | collective-permute-start | bytes 200 | tf_op jit(solution)/shard_map/ppermute | solution.py:20
  14.5 1.6 %shard_map.87 = (f32[24,64,128]{2,1,0:T(8,128)S(1)}, f32[24,64,128]{2,1,0:T(8,128)S(1)}, f32[12,64,128]{2,1,0:T(8,128)S(1)}, f32[12,64,128]{2,1,0:T(8,128)S(1)}) custom-call(s32[8,2]{1,0:T(8,128)S(1)} %copy.15.own.offsets, s32[8,2]{1,0:T(8,128)S(1)} %collective-permute-done.1.far, s32[1]{0:T(128)S(6)} %copy.18.counts, f32[4,64,2048]{2,1,0:T(8,128)S(1)} %bitcast.11, ...), custom_call_target="tpu_custom_call" | custom-call | bytes 4194304 | tf_op jit(solution)/shard_map/pallas_call | solution.py:269
  16.1 0.5 collective-permute-start.6
  16.6 0.0 collective-permute-start.7
  16.6 0.0 copy-done.4
  16.6 0.2 cosine_bitcast_fusion
  16.8 13.4 %collective-permute-done.offsets.middle = s32[8,2]{1,0:T(8,128)S(1)} collective-permute-done((s32[8,2]{1,0:T(8,128)S(1)}, s32[8,2]{1,0:T(8,128)S(1)}, u32[]{:S(2)}, u32[]{:S(2)}) %collective-permute-start) | collective-permute-done | bytes 96 | tf_op jit(solution)/shard_map/ppermute | solution.py:20
  30.2 0.0 collective-permute-done.2.near
  30.2 2.5 %collective-permute-done.3.cross = f32[12,64,128]{2,1,0:T(8,128)S(1)} collective-permute-done((f32[12,64,128]{2,1,0:T(8,128)S(1)}, f32[12,64,128]{2,1,0:T(8,128)S(1)}, u32[]{:S(2)}, u32[]{:S(2)}) %collective-permute-start.3) | collective-permute-done | bytes 393248 | tf_op jit(solution)/shard_map/ppermute | solution.py:280
  32.7 0.0 copy-done.2
  32.7 0.0 copy-done.3
  32.7 11.1 %shard_map.88 = (f32[20,64,128]{2,1,0:T(8,128)S(1)}, f32[8,64,128]{2,1,0:T(8,128)S(1)}, f32[20,64,128]{2,1,0:T(8,128)S(1)}, f32[9,128,128]{2,1,0:T(8,128)S(1)}) custom-call(s32[8,2]{1,0:T(8,128)S(1)} %collective-permute-done.offsets.middle, f32[4,64,2048]{2,1,0:T(8,128)} %bitcast.7, f32[12,64,128]{2,1,0:T(8,128)S(1)} %collective-permute-done.2.near, ...), custom_call_target="tpu_custom_call" | custom-call | flops 4831838208 | bytes 8388608 | tf_op jit(solution)/shard_map/pallas_call | solution.py:299
  43.8 0.1 collective-permute-start.4
  43.9 0.1 collective-permute-start.5
  44.0 0.0 collective-permute-done.6.near
  44.0 0.0 collective-permute-done.7.cross
  44.0 2.0 %shard_map.89 = (f32[16,64,128]{2,1,0:T(8,128)S(1)}, f32[16,64,128]{2,1,0:T(8,128)S(1)}, f32[16,64,128]{2,1,0:T(8,128)S(1)}, f32[9,128,128]{2,1,0:T(8,128)S(1)}) custom-call(s32[8,2]{1,0:T(8,128)S(1)} %collective-permute-done.offsets.middle, f32[4,64,2048]{2,1,0:T(8,128)} %bitcast.8, f32[24,64,128]{2,1,0:T(8,128)S(1)} %collective-permute-done.6.near, ...), custom_call_target="tpu_custom_call" | custom-call | flops 9663676416 | bytes 8388608 | tf_op jit(solution)/shard_map/pallas_call | solution.py:299
  46.0 19.8 %collective-permute-start.9 = (f32[16,64,128]{2,1,0:T(8,128)S(1)}, f32[16,64,128]{2,1,0:T(8,128)S(1)}, u32[]{:S(2)}, u32[]{:S(2)}) collective-permute-start(f32[16,64,128]{2,1,0:T(8,128)S(1)} %get-tuple-element.40), channel_id=1, source_target_pairs={{0,1},{1,0},{2,3},{3,2},{4,5},{5,4},{6,7},{7,6},{8,9},{9,8},{10,11... | collective-permute-start | bytes 1572872 | tf_op jit(solution)/shard_map/ppermute | solution.py:280
  65.8 0.0 collective-permute-start.10
  65.8 0.0 collective-permute-done.4.near.refs_3_
  65.8 0.0 collective-permute-done.5.cross.refs_4_
  65.8 2.9 %shard_map.90 = (f32[8,64,128]{2,1,0:T(8,128)S(1)}, f32[8,64,128]{2,1,0:T(8,128)S(1)}, f32[8,64,128]{2,1,0:T(8,128)S(1)}, f32[9,128,128]{2,1,0:T(8,128)}, f32[8,...) custom-call(s32[8,2]{1,0:T(8,128)S(1)} %collective-permute-done.offsets.middle, f32[4,64,2048]{2,1,0:T(8,128)} %bitcast.9, ...), custom_call_target="tpu_custom_call" | custom-call | flops 4831838208 | bytes 8388608 | tf_op jit(solution)/shard_map/pallas_call | solution.py:299
  68.7 3.3 %collective-permute-start.8 = (f32[8,9,8,128]{3,2,1,0:T(8,128)S(1)}, f32[8,9,8,128]{3,2,1,0:T(8,128)S(1)}, u32[]{:S(2)}, u32[]{:S(2)}) collective-permute-start(f32[8,9,8,128]{3,2,1,0:T(8,128)S(1)} %get-tuple-element.36), channel_id=1, source_target_pairs={{0,1},{1,0},{2,3},{3,2},{4,5},{5,4},{6,7},{7,6},{8,9},{9,8},{10,11... | collective-permute-start | bytes 884744 | tf_op jit(solution)/shard_map/ppermute | solution.py:329
  72.0 0.0 collective-permute-start.11
  72.0 0.0 collective-permute-start.12
  72.0 0.0 collective-permute-done.9.refs_5_
  72.0 8.0 %collective-permute-done.10.refs_6_ = f32[16,64,128]{2,1,0:T(8,128)S(1)} collective-permute-done((f32[16,64,128]{2,1,0:T(8,128)S(1)}, f32[16,64,128]{2,1,0:T(8,128)S(1)}, u32[]{:S(2)}, u32[]{:S(2)}) %collective-permute-start.10) | collective-permute-done | bytes 524320 | tf_op jit(solution)/shard_map/ppermute | solution.py:280
  80.1 5.0 %shard_map.91.refs_2_ = f32[4,64,2048]{2,1,0:T(8,128)} custom-call(s32[8,2]{1,0:T(8,128)S(1)} %copy.15.own.offsets, s32[8,2]{1,0:T(8,128)S(1)} %collective-permute-done.offsets.middle, s32[8,2]{1,0:T(8,128)S(1)} %collective-permute-done.1.far, f32[8,64,128]{2,1,0:T(8,128)S(1)} %get-tuple-element.37.refs_0_, f32[16,64,128]{2,1,0:T(8,128)S(1)} %get-tuple-element.38.refs_1_, ...), custom_call_target="tpu_custom_call" | custom-call | bytes 5242880 | tf_op jit(solution)/shard_map/pallas_call | solution.py:317
  85.0 0.0 collective-permute-done.8
  85.1 0.0 collective-permute-done.11.refs_0_
  85.1 0.0 collective-permute-done.12.refs_1_
  85.1 16.2 %all_to_all.10.parts = f32[8,9,8,128]{3,2,1,0:T(8,128)S(1)} all-to-all(f32[8,9,8,128]{3,2,1,0:T(8,128)S(1)} %add.3), channel_id=1, replica_groups={{0,2,4,6,8,10,12,14},{1,3,5,7,9,11,13,15},{16,18,20,22,24,26,28,30},{17..., dimensions={0} | all-to-all | bytes 589824 | tf_op jit(solution)/shard_map/all_to_all | solution.py:333
  101.3 10.3 %all_to_all.11.own = f32[8,8,8,128]{3,2,1,0:T(8,128)S(1)} all-to-all(f32[8,8,8,128]{3,2,1,0:T(8,128)S(1)} %shard_map.93), channel_id=1, replica_groups={{0,2,4,6,8,10,12,14},{1,3,5,7,9,11,13,15},{16,18,20,22,24,26,28,30},{17..., dimensions={0} | all-to-all | bytes 524288 | tf_op jit(solution)/shard_map/all_to_all | solution.py:341
  111.6 2.0 %collective-permute-start.13 = (f32[8,8,8,128]{3,2,1,0:T(8,128)S(1)}, f32[8,8,8,128]{3,2,1,0:T(8,128)S(1)}, u32[]{:S(2)}, u32[]{:S(2)}) collective-permute-start(f32[8,8,8,128]{3,2,1,0:T(8,128)S(1)} %all_to_all.11.own), channel_id=1, source_target_pairs={{0,1},{1,0},{2,3},{3,2},{4,5},{5,4},{6,7},{7,6},{8,9},{9,8},{10,11... | collective-permute-start | bytes 786440 | tf_op jit(solution)/shard_map/ppermute | solution.py:352
  113.6 3.6 %shard_map.92 = f32[4,64,2048]{2,1,0:T(8,128)} custom-call(s32[8,2]{1,0:T(8,128)S(1)} %copy.15.own.offsets, s32[8,2]{1,0:T(8,128)S(1)} %collective-permute-done.offsets.middle, s32[8,2]{1,0:T(8,128)S(1)} %collective-permute-done.1.far, f32[8,64,128]{2,1,0:T(8,128)S(1)} %collective-permute-done.11.refs_0_, ...), custom_call_target="tpu_custom_call", output_to_operand_aliasing={{}: (5, {})} | custom-call | bytes 5242880 | tf_op jit(solution)/shard_map/pallas_call | solution.py:317
  117.2 0.0 collective-permute-done.13.other
  117.2 1.5 %shard_map.94 = f32[8,128,128]{2,1,0:T(8,128)} custom-call(s32[8,2]{1,0:T(8,128)S(1)} %copy.15.own.offsets, f32[8,8,8,128]{3,2,1,0:T(8,128)S(1)} %all_to_all.11.own, f32[8,8,8,128]{3,2,1,0:T(8,128)S(1)} %collective-permute-done.13.other), custom_call_target="tpu_custom_call" | custom-call | tf_op jit(solution)/shard_map/pallas_call | solution.py:346
  (6 shorter events, 0.1 us)
Async XLA Ops:
  1.4 6.1 %collective-permute-start.1 = (s32[8,2]{1,0:T(8,128)S(1)}, s32[8,2]{1,0:T(8,128)S(1)}, u32[]{:S(2)}, u32[]{:S(2)}) collective-permute-start(s32[8,2]{1,0:T(8,128)S(1)} %copy.15.own.offsets), channel_id=1, source_target_pairs={{0,2},{1,3},{2,4},{3,5},{4,6},{5,7},{6,8},{7,9},{8,10},{9,11},{10,... | collective-permute-start | bytes 200 | tf_op jit(solution)/shard_map/ppermute | solution.py:20
  7.5 1.6 %copy-start = (f32[2,2,64,2048]{3,2,1,0:T(8,128)S(1)}, f32[2,2,64,2048]{3,2,1,0:T(8,128)}, u32[]{:S(2)}) copy-start(f32[2,2,64,2048]{3,2,1,0:T(8,128)} %param.7) | copy-start | bytes 6291460
  9.1 1.0 copy-start.1
  10.1 6.5 %copy-start.4 = (f32[128,128]{1,0:T(8,128)S(1)}, f32[128,128]{1,0:T(8,128)}, u32[]{:S(2)}) copy-start(f32[128,128]{1,0:T(8,128)} %param.9) | copy-start | bytes 196612
  11.1 21.6 %copy-start.2 = (f32[4,2,128,128]{3,2,1,0:T(8,128)S(1)}, f32[4,2,128,128]{3,2,1,0:T(8,128)}, u32[]{:S(2)}) copy-start(f32[4,2,128,128]{3,2,1,0:T(8,128)} %probe.5) | copy-start | bytes 1572868
  11.2 21.6 %copy-start.3 = (bf16[4,256,256]{2,1,0:T(8,128)(2,1)S(1)}, bf16[4,256,256]{2,1,0:T(8,128)(2,1)}, u32[]{:S(2)}) copy-start(bf16[4,256,256]{2,1,0:T(8,128)(2,1)} %constant.4.clone.tables) | copy-start | bytes 1572868
  11.2 19.0 %collective-permute-start.2 = (f32[12,64,128]{2,1,0:T(8,128)S(1)}, f32[12,64,128]{2,1,0:T(8,128)S(1)}, u32[]{:S(2)}, u32[]{:S(2)}) collective-permute-start(f32[12,64,128]{2,1,0:T(8,128)S(1)} %get-tuple-element.25), channel_id=1, source_target_pairs={{0,1},{1,0},{2,3},{3,2},{4,5},{5,4},{6,7},{7,6},{8,9},{9,8},{10,11... | collective-permute-start | bytes 1179656 | tf_op jit(solution)/shard_map/ppermute | solution.py:280
  12.8 19.9 %collective-permute-start.3 = (f32[12,64,128]{2,1,0:T(8,128)S(1)}, f32[12,64,128]{2,1,0:T(8,128)S(1)}, u32[]{:S(2)}, u32[]{:S(2)}) collective-permute-start(f32[12,64,128]{2,1,0:T(8,128)S(1)} %get-tuple-element.26), channel_id=1, source_target_pairs={{0,15},{1,2},{2,1},{3,4},{4,3},{5,6},{6,5},{7,8},{8,7},{9,10},{10,... | collective-permute-start | bytes 1179656 | tf_op jit(solution)/shard_map/ppermute | solution.py:280
  12.8 17.4 %collective-permute-start = (s32[8,2]{1,0:T(8,128)S(1)}, s32[8,2]{1,0:T(8,128)S(1)}, u32[]{:S(2)}, u32[]{:S(2)}) collective-permute-start(s32[8,2]{1,0:T(8,128)S(1)} %copy.15.own.offsets), channel_id=1, source_target_pairs={{0,1},{1,2},{2,3},{3,4},{4,5},{5,6},{6,7},{7,8},{8,9},{9,10},{10,1... | collective-permute-start | bytes 200 | tf_op jit(solution)/shard_map/ppermute | solution.py:20
  16.1 27.9 %collective-permute-start.6 = (f32[24,64,128]{2,1,0:T(8,128)S(1)}, f32[24,64,128]{2,1,0:T(8,128)S(1)}, u32[]{:S(2)}, u32[]{:S(2)}) collective-permute-start(f32[24,64,128]{2,1,0:T(8,128)S(1)} %get-tuple-element.31), channel_id=1, source_target_pairs={{0,1},{1,0},{2,3},{3,2},{4,5},{5,4},{6,7},{7,6},{8,9},{9,8},{10,11... | collective-permute-start | bytes 2359304 | tf_op jit(solution)/shard_map/ppermute | solution.py:280
  16.6 27.4 %collective-permute-start.7 = (f32[24,64,128]{2,1,0:T(8,128)S(1)}, f32[24,64,128]{2,1,0:T(8,128)S(1)}, u32[]{:S(2)}, u32[]{:S(2)}) collective-permute-start(f32[24,64,128]{2,1,0:T(8,128)S(1)} %get-tuple-element.32), channel_id=1, source_target_pairs={{0,15},{1,2},{2,1},{3,4},{4,3},{5,6},{6,5},{7,8},{8,7},{9,10},{10,... | collective-permute-start | bytes 2359304 | tf_op jit(solution)/shard_map/ppermute | solution.py:280
  43.8 22.0 %collective-permute-start.4 = (f32[20,64,128]{2,1,0:T(8,128)S(1)}, f32[20,64,128]{2,1,0:T(8,128)S(1)}, u32[]{:S(2)}, u32[]{:S(2)}) collective-permute-start(f32[20,64,128]{2,1,0:T(8,128)S(1)} %get-tuple-element.29), channel_id=1, source_target_pairs={{0,1},{1,0},{2,3},{3,2},{4,5},{5,4},{6,7},{7,6},{8,9},{9,8},{10,11... | collective-permute-start | bytes 1966088 | tf_op jit(solution)/shard_map/ppermute | solution.py:280
  43.9 21.9 %collective-permute-start.5 = (f32[20,64,128]{2,1,0:T(8,128)S(1)}, f32[20,64,128]{2,1,0:T(8,128)S(1)}, u32[]{:S(2)}, u32[]{:S(2)}) collective-permute-start(f32[20,64,128]{2,1,0:T(8,128)S(1)} %get-tuple-element.30), channel_id=1, source_target_pairs={{0,15},{1,2},{2,1},{3,4},{4,3},{5,6},{6,5},{7,8},{8,7},{9,10},{10,... | collective-permute-start | bytes 1966088 | tf_op jit(solution)/shard_map/ppermute | solution.py:280
  46.0 26.0 %collective-permute-start.9 = (f32[16,64,128]{2,1,0:T(8,128)S(1)}, f32[16,64,128]{2,1,0:T(8,128)S(1)}, u32[]{:S(2)}, u32[]{:S(2)}) collective-permute-start(f32[16,64,128]{2,1,0:T(8,128)S(1)} %get-tuple-element.40), channel_id=1, source_target_pairs={{0,1},{1,0},{2,3},{3,2},{4,5},{5,4},{6,7},{7,6},{8,9},{9,8},{10,11... | collective-permute-start | bytes 1572872 | tf_op jit(solution)/shard_map/ppermute | solution.py:280
  65.8 14.2 %collective-permute-start.10 = (f32[16,64,128]{2,1,0:T(8,128)S(1)}, f32[16,64,128]{2,1,0:T(8,128)S(1)}, u32[]{:S(2)}, u32[]{:S(2)}) collective-permute-start(f32[16,64,128]{2,1,0:T(8,128)S(1)} %get-tuple-element.41), channel_id=1, source_target_pairs={{0,15},{1,2},{2,1},{3,4},{4,3},{5,6},{6,5},{7,8},{8,7},{9,10},{10,... | collective-permute-start | bytes 1572872 | tf_op jit(solution)/shard_map/ppermute | solution.py:280
  68.7 16.3 %collective-permute-start.8 = (f32[8,9,8,128]{3,2,1,0:T(8,128)S(1)}, f32[8,9,8,128]{3,2,1,0:T(8,128)S(1)}, u32[]{:S(2)}, u32[]{:S(2)}) collective-permute-start(f32[8,9,8,128]{3,2,1,0:T(8,128)S(1)} %get-tuple-element.36), channel_id=1, source_target_pairs={{0,1},{1,0},{2,3},{3,2},{4,5},{5,4},{6,7},{7,6},{8,9},{9,8},{10,11... | collective-permute-start | bytes 884744 | tf_op jit(solution)/shard_map/ppermute | solution.py:329
  72.0 13.1 %collective-permute-start.11 = (f32[8,64,128]{2,1,0:T(8,128)S(1)}, f32[8,64,128]{2,1,0:T(8,128)S(1)}, u32[]{:S(2)}, u32[]{:S(2)}) collective-permute-start(f32[8,64,128]{2,1,0:T(8,128)S(1)} %get-tuple-element.42), channel_id=1, source_target_pairs={{0,1},{1,0},{2,3},{3,2},{4,5},{5,4},{6,7},{7,6},{8,9},{9,8},{10,11... | collective-permute-start | bytes 786440 | tf_op jit(solution)/shard_map/ppermute | solution.py:280
  72.0 13.1 %collective-permute-start.12 = (f32[8,64,128]{2,1,0:T(8,128)S(1)}, f32[8,64,128]{2,1,0:T(8,128)S(1)}, u32[]{:S(2)}, u32[]{:S(2)}) collective-permute-start(f32[8,64,128]{2,1,0:T(8,128)S(1)} %get-tuple-element.43), channel_id=1, source_target_pairs={{0,15},{1,2},{2,1},{3,4},{4,3},{5,6},{6,5},{7,8},{8,7},{9,10},{10,... | collective-permute-start | bytes 786440 | tf_op jit(solution)/shard_map/ppermute | solution.py:280
  111.6 5.6 %collective-permute-start.13 = (f32[8,8,8,128]{3,2,1,0:T(8,128)S(1)}, f32[8,8,8,128]{3,2,1,0:T(8,128)S(1)}, u32[]{:S(2)}, u32[]{:S(2)}) collective-permute-start(f32[8,8,8,128]{3,2,1,0:T(8,128)S(1)} %all_to_all.11.own), channel_id=1, source_target_pairs={{0,1},{1,0},{2,3},{3,2},{4,5},{5,4},{6,7},{7,6},{8,9},{9,8},{10,11... | collective-permute-start | bytes 786440 | tf_op jit(solution)/shard_map/ppermute | solution.py:352

commit v2 on v1

--- a/solution.py
+++ b/solution.py
@@ -36,25 +36,31 @@
     return high, (array - high.astype(F32)).astype(BF16)
 
 
-def transform(tables, conj, waves):
+def transform(tables, conj, groups):
     at_left, at_right = (2, 0) if conj else (0, 2)
     left = jnp.concatenate([tables[at_left], tables[at_left + 1], tables[at_left]], axis=1)
     right = jnp.concatenate([tables[at_right], tables[at_right], tables[at_right + 1]], axis=0)
-    stacked = jnp.concatenate([jnp.concatenate(wave, axis=0) for wave in waves], axis=1)
-    high, low = pieces(stacked)
-    half = jnp.dot(left, jnp.concatenate([high, high, low], axis=0), preferred_element_type=F32)
-    pixels = half.shape[0] // 2
-    places = [i * pixels for i in range(len(waves))]
-    turned = jnp.concatenate(
-        [
+    pixels = left.shape[0] // 2
+    halves = []
+    for waves in groups:
+        stacked = jnp.concatenate([jnp.concatenate(wave, axis=0) for wave in waves], axis=1)
+        high, low = pieces(stacked)
+        half = jnp.dot(left, jnp.concatenate([high, high, low], axis=0), preferred_element_type=F32)
+        turned = [
             jnp.concatenate([half[:pixels, at : at + pixels], half[pixels:, at : at + pixels]], axis=1)
-            for at in places
-        ],
-        axis=0,
-    )
-    high, low = pieces(turned)
-    whole = jnp.dot(jnp.concatenate([high, low, high], axis=1), right, preferred_element_type=F32)
-    return [(whole[at : at + pixels, :pixels], whole[at : at + pixels, pixels:]) for at in places]
+            for at in range(0, half.shape[1], pixels)
+        ]
+        halves.append(pieces(jnp.concatenate(turned, axis=0)))
+    wholes = []
+    for high, low in halves:
+        whole = jnp.dot(jnp.concatenate([high, low, high], axis=1), right, preferred_element_type=F32)
+        wholes.append(
+            [
+                (whole[at : at + pixels, :pixels], whole[at : at + pixels, pixels:])
+                for at in range(0, whole.shape[0], pixels)
+            ]
+        )
+    return wholes
 
 
 def times(one, two):
@@ -95,6 +101,12 @@
             target = (measured[slot] * live).reshape(-1, rows, pixels)
             near[strip + planes : strip + planes + pixels // rows] = target
             cross[strip + planes : strip + planes + pixels // rows] = target
+        if first == 0:
+            for slot in range(measured.shape[0]):
+                for entry in range(2):
+                    line = jnp.full((1, pixels), own[slot, entry], jnp.int32).astype(F32)
+                    near[near.shape[0] - 1, 2 * slot + entry : 2 * slot + entry + 1] = line
+                    cross[cross.shape[0] - 1, 2 * slot + entry : 2 * slot + entry + 1] = line
 
 
 def add_kernel(pixels, groups, own, middle, far, *refs):
@@ -126,8 +138,13 @@
 
 
 def slot_kernel(
-    first, size, ahead, offsets, tile, near, cross, probe, prop, tables, so_far, *refs
+    first, size, ahead, own_offsets, *refs
 ):
+    if first == 0:
+        offsets, refs = refs[-6], refs[:-6] + refs[-5:]
+    else:
+        offsets, *refs = refs
+    tile, near, cross, probe, prop, tables, so_far, *refs = refs
     given, refs = refs[:ahead], refs[ahead:]
     out_near, out_mid, out_cross, total, *shares = refs[:-5]
     window, patch, grads, exit_wave, far = refs[-5:]
@@ -137,9 +154,15 @@
     behind = given[0].shape[0] if given else 0
     for message, out in zip(given, (out_near, out_cross)):
         out[:behind] = message[...]
-    even = jnp.logical_not(is_even(offsets, rows))
+    even = is_even(own_offsets, rows)
+    if first == 0:
+        for slot in range(offsets.shape[0]):
+            for entry in range(2):
+                line = pl.ds(2 * slot + entry, 1)
+                value = jnp.where(even, cross[cross.shape[0] - 1, line], near[near.shape[0] - 1, line])
+                offsets[slot, entry] = jnp.max(value).astype(jnp.int32)
     total[...] = so_far[...]
-    held = [(s, m) for s in range(BATCH) for m in range(modes)]
+    held = range(BATCH)
 
     def is_live(at):
         unit = at * each + planes
@@ -160,39 +183,48 @@
             window[:, 2 * rows :] = jnp.where(even, near[strip], cross[strip])
             patch[s] = window[:, pl.ds(starts[s], pixels), :]
             total[2 * modes] += live[s] * (patch[s, 0] * patch[s, 0] + patch[s, 1] * patch[s, 1])
-        waves = [times((probe[m, 0], probe[m, 1]), (patch[s, 0], patch[s, 1])) for s, m in held]
-        waves = transform(tables, False, waves)
-        waves = [times((prop[0], prop[1]), wave) for wave in waves]
-        waves = transform(tables, True, waves)
-        for (s, m), wave in zip(held, waves):
-            exit_wave[s, m, 0], exit_wave[s, m, 1] = wave
-        waves = [times(wave, (patch[s, 2], patch[s, 3])) for (s, m), wave in zip(held, waves)]
-        waves = transform(tables, False, waves)
-        intensity = [jnp.zeros((pixels, pixels), F32)] * BATCH
-        for (s, m), wave in zip(held, waves):
-            far[s, m, 0], far[s, m, 1] = wave
-            intensity[s] = intensity[s] + wave[0] * wave[0] + wave[1] * wave[1]
-        units = [pl.ds(at * each + planes, each - planes) for at in slots]
-        target = [jnp.where(even, cross[unit], near[unit]).reshape(pixels, pixels) for unit in units]
-        misfit = [2.0 * live[s] * (intensity[s] - target[s]) for s in range(BATCH)]
-        waves = [(misfit[s] * far[s, m, 0], misfit[s] * far[s, m, 1]) for s, m in held]
-        waves = transform(tables, True, waves)
-        grads[...] = jnp.zeros_like(grads)
-        for (s, m), wave in zip(held, waves):
-            re, im = conj_times((exit_wave[s, m, 0], exit_wave[s, m, 1]), wave)
-            grads[s, 2] += re
-            grads[s, 3] += im
-        waves = [conj_times((patch[s, 2], patch[s, 3]), wave) for (s, m), wave in zip(held, waves)]
-        waves = transform(tables, False, waves)
-        waves = [conj_times((prop[0], prop[1]), wave) for wave in waves]
-        waves = transform(tables, True, waves)
-        for (s, m), wave in zip(held, waves):
-            re, im = conj_times((patch[s, 0], patch[s, 1]), wave)
-            total[2 * m] += re
-            total[2 * m + 1] += im
-            re, im = conj_times((probe[m, 0], probe[m, 1]), wave)
-            grads[s, 0] += re
-            grads[s, 1] += im
+        all_modes = range(modes)
+        groups = [
+            [times((probe[m, 0], probe[m, 1]), (patch[s, 0], patch[s, 1])) for m in all_modes] for s in held
+        ]
+        groups = transform(tables, False, groups)
+        groups = [[times((prop[0], prop[1]), wave) for wave in waves] for waves in groups]
+        groups = transform(tables, True, groups)
+        for s in held:
+            for m in all_modes:
+                exit_wave[s, m, 0], exit_wave[s, m, 1] = groups[s][m]
+            groups[s] = [times(wave, (patch[s, 2], patch[s, 3])) for wave in groups[s]]
+        groups = transform(tables, False, groups)
+        for s, at in enumerate(slots):
+            intensity = jnp.zeros((pixels, pixels), F32)
+            for m in all_modes:
+                wave = groups[s][m]
+                far[s, m, 0], far[s, m, 1] = wave
+                intensity = intensity + wave[0] * wave[0] + wave[1] * wave[1]
+            unit = pl.ds(at * each + planes, each - planes)
+            target = jnp.where(even, cross[unit], near[unit]).reshape(pixels, pixels)
+            misfit = 2.0 * live[s] * (intensity - target)
+            groups[s] = [(misfit * far[s, m, 0], misfit * far[s, m, 1]) for m in all_modes]
+        groups = transform(tables, True, groups)
+        for s in held:
+            grad_re, grad_im = jnp.zeros((pixels, pixels), F32), jnp.zeros((pixels, pixels), F32)
+            for m in all_modes:
+                re, im = conj_times((exit_wave[s, m, 0], exit_wave[s, m, 1]), groups[s][m])
+                grad_re, grad_im = grad_re + re, grad_im + im
+            grads[s, 2], grads[s, 3] = grad_re, grad_im
+            groups[s] = [conj_times((patch[s, 2], patch[s, 3]), wave) for wave in groups[s]]
+        groups = transform(tables, False, groups)
+        groups = [[conj_times((prop[0], prop[1]), wave) for wave in waves] for waves in groups]
+        groups = transform(tables, True, groups)
+        for s in held:
+            grad_re, grad_im = jnp.zeros((pixels, pixels), F32), jnp.zeros((pixels, pixels), F32)
+            for m in all_modes:
+                re, im = conj_times((patch[s, 0], patch[s, 1]), groups[s][m])
+                total[2 * m] += re
+                total[2 * m + 1] += im
+                re, im = conj_times((probe[m, 0], probe[m, 1]), groups[s][m])
+                grad_re, grad_im = grad_re + re, grad_im + im
+            grads[s, 0], grads[s, 1] = grad_re, grad_im
         for s, at in enumerate(slots):
             window[...] = jnp.zeros_like(window)
             window[:, pl.ds(starts[s], pixels), :] = grads[s]
@@ -257,7 +289,6 @@
     pair = [(i, i ^ 1) for i in range(peers)]
     other_pair = [(i, (i - 1) % peers if i % 2 == 0 else (i + 1) % peers) for i in range(peers)]
     far = shifted(offsets, "row", 2)
-    middle = shifted(offsets, "row", 1)
 
     each = planes + pixels // tile_rows
 
@@ -265,7 +296,7 @@
         return jax.ShapeDtypeStruct((count, tile_rows, pixels), F32)
 
     def strips(chunks):
-        shapes = [units(size * each) for _, size in chunks for _ in range(2)]
+        shapes = [units(size * each + (first == 0)) for first, size in chunks for _ in range(2)]
         outs = pl.pallas_call(
             functools.partial(cut_kernel, pixels, chunks),
             out_shape=shapes,
@@ -287,7 +318,7 @@
 
     share = pixels // peers
     total = jnp.zeros((2 * modes + 1, pixels, pixels), F32)
-    mid, back = [], []
+    mid, back, places = [], [], [offsets]
     for index, (first, size) in enumerate(chunks):
         given = waiting[index + 2] if index + 2 < len(chunks) else ()
         ahead = CHUNKS[index + 2] * each if given else 0
@@ -298,15 +329,20 @@
         kept = pltpu.VMEM((BATCH, modes, 2, pixels, pixels), F32)
         to_near, to_mid, to_cross, total, *shares = pl.pallas_call(
             functools.partial(slot_kernel, first, size, len(given)),
-            out_shape=[message, units(size * planes), message, jax.ShapeDtypeStruct(total.shape, F32)] + shares,
-            in_specs=[in_smem()] + [in_vmem()] * (7 + len(given)),
-            out_specs=[in_vmem()] * (4 + len(shares)),
+            out_shape=[message, units(size * planes), message, jax.ShapeDtypeStruct(total.shape, F32)]
+            + shares
+            + ([] if index else [jax.ShapeDtypeStruct(offsets.shape, jnp.int32)]),
+            in_specs=[in_smem()] * len(places) + [in_vmem()] * (7 + len(given)),
+            out_specs=[in_vmem()] * (4 + len(shares)) + ([] if index else [in_smem()]),
             scratch_shapes=[pltpu.VMEM((planes, 3 * tile_rows, pixels), F32), field, field, kept, kept],
             compiler_params=params,
             cost_estimate=pl.CostEstimate(
                 flops=size * 6 * modes * 3 * 16 * pixels**3, bytes_accessed=8 << 20, transcendentals=0
             ),
-        )(middle, tile, *arrived[index], probe_modes, prop, tables, total, *given)
+        )(*places, tile, *arrived[index], probe_modes, prop, tables, total, *given)
+        if index == 0:
+            middle = shares.pop()
+            places.append(middle)
         mid.append((("mid", first, size, 0), to_mid))
         message = swapped(to_near, to_cross)
         if given:

time: 120 us -> 112 us (0.933)
  starting transfers between devices: 31.1 us -> 12.3 us
  Pallas kernels: 28.7 us -> 46.3 us
  waiting for transfers between devices: 27.3 us -> 23.9 us
  blocking collectives: 26.5 us -> 23.7 us
    pallas_call x3, Pallas kernels: 16 us -> 33.6 us  [local(): pl.pallas_call(functools.partial(slot_kernel, first, size, len(given)), o...]
    ppermute x5, starting transfers between devices: 22 us -> 6.05 us  [swapped(): lax.ppermute(to_near, 'row', pair)]
    ppermute x2 -> x1, waiting for transfers between devices: 16.7 us -> 3.38 us  [shifted(): lax.ppermute(array, axis, [(i, (i + by) % peers) for i in range(peers)])]
    ppermute x5, waiting for transfers between devices: 10.5 us -> 20.5 us  [swapped(): lax.ppermute(to_cross, 'row', other_pair)]
    all_to_all x1, blocking collectives: 16.2 us -> 12.3 us  [local(): parts = lax.all_to_all(both, 'row', 0, 0, axis_index_groups=cores)]
    ppermute x2 -> x1, starting transfers between devices: 3.81 us -> 2.07 us  [shifted(): lax.ppermute(array, axis, [(i, (i + by) % peers) for i in range(peers)])]
    ppermute x1, starting transfers between devices: 3.26 us -> 1.53 us  [local(): both = own + lax.ppermute(other, 'row', pair)]
  transfers between devices with their start and end apart: 14 -> 13, of which waited for: 4 -> 4; matrix products, arithmetic and copies ran while one was open for 0% -> 0% of each run, Pallas kernels for 22% -> 39%
where the time goes in v2:
time: 112 us; the launch traced here: 111 us
  Pallas kernels  46.3 us (41%)
  waiting for transfers between devices  23.9 us (21%)
  blocking collectives  23.7 us (21%)
  starting transfers between devices  12.3 us (11%)
  local copies, waits for them, and re-layouts  3.68 us (3%)
  between operations  1.44 us (1%)
    pallas_call x3, Pallas kernels, local(): pl.pallas_call(functools.partial(slot_kernel, first, size, len(given)), o...  33.6 us
    ppermute x5, waiting for transfers between devices, swapped(): lax.ppermute(to_cross, 'row', other_pair)  20.5 us
    all_to_all x1, blocking collectives, local(): parts = lax.all_to_all(both, 'row', 0, 0, axis_index_groups=cores)  12.3 us
    all_to_all x1, blocking collectives, local(): gathered = lax.all_to_all(spread, 'row', 0, 0, axis_index_groups=cores)  11.3 us
    pallas_call x2, Pallas kernels, added(): pl.pallas_call(functools.partial(add_kernel, pixels, groups), out_shape=j...  8.6 us
    ppermute x5, starting transfers between devices, swapped(): lax.ppermute(to_near, 'row', pair)  6.05 us
    unnamed x11, local copies, waits for them, and re-layouts  3.4 us
    ppermute x1, waiting for transfers between devices, shifted(): lax.ppermute(array, axis, [(i, (i + by) % peers) for i in range(peers)])  3.38 us
  transfers between devices with their start and end apart: 13, of which 4 were waited for; matrix products, arithmetic and copies ran while one was open for 0% of the time, Pallas kernels for 39%

profile of v2, /device:TPU:1, one launch (start us, length us, event | category | flops | bytes accessed | tf_op | source)
XLA Modules:
  0.0 111.4 jit_solution(5803185888599205413)
XLA Ops:
  0.6 0.8 copy.17.own.own_offsets.offsets
  1.4 2.1 %collective-permute-start = (s32[8,2]{1,0:T(8,128)S(1)}, s32[8,2]{1,0:T(8,128)S(1)}, u32[]{:S(2)}, u32[]{:S(2)}) collective-permute-start(s32[8,2]{1,0:T(8,128)S(1)} %copy.17.own.own_offsets.offsets), channel_id=1, source_target_pairs={{0,2},{1,3},{2,4},{3,5},{4,6},{5,7},{6,8},{7,9},{8,10},{9,11},{10,... | collective-permute-start | bytes 200 | tf_op jit(solution)/shard_map/ppermute | solution.py:20
  4.1 3.4 %collective-permute-done.far = s32[8,2]{1,0:T(8,128)S(1)} collective-permute-done((s32[8,2]{1,0:T(8,128)S(1)}, s32[8,2]{1,0:T(8,128)S(1)}, u32[]{:S(2)}, u32[]{:S(2)}) %collective-permute-start) | collective-permute-done | bytes 96 | tf_op jit(solution)/shard_map/ppermute | solution.py:20
  7.5 0.0 copy-start
  7.5 1.6 %copy-done = f32[2,2,64,2048]{3,2,1,0:T(8,128)S(1)} copy-done((f32[2,2,64,2048]{3,2,1,0:T(8,128)S(1)}, f32[2,2,64,2048]{3,2,1,0:T(8,128)}, u32[]{:S(2)}) %copy-start) | copy-done | bytes 2097176
  9.1 0.0 copy-start.1
  9.1 1.0 copy-done.1
  10.1 0.0 copy-start.4
  10.1 1.0 shard_map.86
  11.1 0.0 copy-start.2
  11.2 0.0 copy-start.3
  11.2 1.6 %collective-permute-start.1 = (f32[13,64,128]{2,1,0:T(8,128)S(1)}, f32[13,64,128]{2,1,0:T(8,128)S(1)}, u32[]{:S(2)}, u32[]{:S(2)}) collective-permute-start(f32[13,64,128]{2,1,0:T(8,128)S(1)} %get-tuple-element.26), channel_id=1, source_target_pairs={{0,1},{1,0},{2,3},{3,2},{4,5},{5,4},{6,7},{7,6},{8,9},{9,8},{10,11... | collective-permute-start | bytes 1277960 | tf_op jit(solution)/shard_map/ppermute | solution.py:311
  12.8 0.0 collective-permute-start.2
  12.8 1.6 %shard_map.87 = (f32[24,64,128]{2,1,0:T(8,128)S(1)}, f32[24,64,128]{2,1,0:T(8,128)S(1)}, f32[12,64,128]{2,1,0:T(8,128)S(1)}, f32[12,64,128]{2,1,0:T(8,128)S(1)}) custom-call(s32[8,2]{1,0:T(8,128)S(1)} %copy.17.own.own_offsets.offsets, s32[8,2]{1,0:T(8,128)S(1)} %collective-permute-done.far, s32[1]{0:T(128)S(6)} %copy.20.counts, f32[4,64,2048]{2,1,0:T(8,128)S(1)} %bitcast.11, ...), custom_call_target="tpu_custom_call" | custom-call | bytes 4194304 | tf_op jit(solution)/shard_map/pallas_call | solution.py:300
  14.4 2.2 %collective-permute-start.5 = (f32[24,64,128]{2,1,0:T(8,128)S(1)}, f32[24,64,128]{2,1,0:T(8,128)S(1)}, u32[]{:S(2)}, u32[]{:S(2)}) collective-permute-start(f32[24,64,128]{2,1,0:T(8,128)S(1)} %get-tuple-element.33), channel_id=1, source_target_pairs={{0,1},{1,0},{2,3},{3,2},{4,5},{5,4},{6,7},{7,6},{8,9},{9,8},{10,11... | collective-permute-start | bytes 2359304 | tf_op jit(solution)/shard_map/ppermute | solution.py:311
  16.6 0.0 collective-permute-start.6
  16.6 0.0 copy-done.4
  16.6 0.2 cosine_bitcast_fusion
  16.8 0.0 collective-permute-done.1.refs_1_
  16.8 16.5 %collective-permute-done.2.refs_2_ = f32[13,64,128]{2,1,0:T(8,128)S(1)} collective-permute-done((f32[13,64,128]{2,1,0:T(8,128)S(1)}, f32[13,64,128]{2,1,0:T(8,128)S(1)}, u32[]{:S(2)}, u32[]{:S(2)}) %collective-permute-start.2) | collective-permute-done | bytes 426016 | tf_op jit(solution)/shard_map/ppermute | solution.py:311
  33.4 0.0 copy-done.2
  33.4 0.0 copy-done.3
  33.4 9.2 %shard_map.88 = (f32[20,64,128]{2,1,0:T(8,128)S(1)}, f32[8,64,128]{2,1,0:T(8,128)S(1)}, f32[20,64,128]{2,1,0:T(8,128)S(1)}, f32[9,128,128]{2,1,0:T(8,128)S(1)}, s32[8,2]{1,0:T(8,128)S(1)}) custom-call(s32[8,2]{1,0:T(8,128)S(1)} %copy.17.own.own_offsets.offsets, f32[4,64,2048]{2,1,0:T(8,128)} %bitcast.7, f32[13,64,128]{2,1,0:T(8,128)S(1)} %collective-permute-done.1.refs_1_, ...), custom_call_target="tpu_custom_call" | custom-call | flops 4831838208 | bytes 8388608 | tf_op jit(solution)/shard_map/pallas_call | solution.py:330
  42.6 0.1 collective-permute-start.3
  42.7 0.1 collective-permute-start.4
  42.8 0.0 collective-permute-done.5.refs_2_
  42.8 0.0 collective-permute-done.6.refs_3_
  42.8 15.1 %shard_map.89 = (f32[16,64,128]{2,1,0:T(8,128)S(1)}, f32[16,64,128]{2,1,0:T(8,128)S(1)}, f32[16,64,128]{2,1,0:T(8,128)S(1)}, f32[9,128,128]{2,1,0:T(8,128)S(1)}) custom-call(s32[8,2]{1,0:T(8,128)S(1)} %copy.17.own.own_offsets.offsets, s32[8,2]{1,0:T(8,128)S(1)} %get-tuple-element.30.refs_0_.middle, f32[4,64,2048]{2,1,0:T(8,128)} %bitcast.8, ...), custom_call_target="tpu_custom_call" | custom-call | flops 9663676416 | bytes 8388608 | tf_op jit(solution)/shard_map/pallas_call | solution.py:330
  58.0 2.2 %collective-permute-start.8 = (f32[16,64,128]{2,1,0:T(8,128)S(1)}, f32[16,64,128]{2,1,0:T(8,128)S(1)}, u32[]{:S(2)}, u32[]{:S(2)}) collective-permute-start(f32[16,64,128]{2,1,0:T(8,128)S(1)} %get-tuple-element.42), channel_id=1, source_target_pairs={{0,1},{1,0},{2,3},{3,2},{4,5},{5,4},{6,7},{7,6},{8,9},{9,8},{10,11... | collective-permute-start | bytes 1572872 | tf_op jit(solution)/shard_map/ppermute | solution.py:311
  60.1 0.0 collective-permute-start.9
  60.1 0.0 collective-permute-done.3.refs_2_.refs_3_
  60.1 0.0 collective-permute-done.4.refs_3_.refs_4_
  60.1 9.3 %shard_map.90 = (f32[8,64,128]{2,1,0:T(8,128)S(1)}, f32[8,64,128]{2,1,0:T(8,128)S(1)}, f32[8,64,128]{2,1,0:T(8,128)S(1)}, f32[9,128,128]{2,1,0:T(8,128)}, f32[8,...) custom-call(s32[8,2]{1,0:T(8,128)S(1)} %copy.17.own.own_offsets.offsets, ...), custom_call_target="tpu_custom_call" | custom-call | flops 4831838208 | bytes 8388608 | tf_op jit(solution)/shard_map/pallas_call | solution.py:330
  69.4 1.5 %collective-permute-start.7 = (f32[8,9,8,128]{3,2,1,0:T(8,128)S(1)}, f32[8,9,8,128]{3,2,1,0:T(8,128)S(1)}, u32[]{:S(2)}, u32[]{:S(2)}) collective-permute-start(f32[8,9,8,128]{3,2,1,0:T(8,128)S(1)} %get-tuple-element.38), channel_id=1, source_target_pairs={{0,1},{1,0},{2,3},{3,2},{4,5},{5,4},{6,7},{7,6},{8,9},{9,8},{10,11... | collective-permute-start | bytes 884744 | tf_op jit(solution)/shard_map/ppermute | solution.py:365
  71.0 0.0 collective-permute-start.10
  71.0 0.0 collective-permute-start.11
  71.0 0.0 collective-permute-done.8.refs_5_
  71.0 3.7 %collective-permute-done.9.refs_6_ = f32[16,64,128]{2,1,0:T(8,128)S(1)} collective-permute-done((f32[16,64,128]{2,1,0:T(8,128)S(1)}, f32[16,64,128]{2,1,0:T(8,128)S(1)}, u32[]{:S(2)}, u32[]{:S(2)}) %collective-permute-start.9) | collective-permute-done | bytes 524320 | tf_op jit(solution)/shard_map/ppermute | solution.py:311
  74.7 5.0 %shard_map.91.refs_2_ = f32[4,64,2048]{2,1,0:T(8,128)} custom-call(s32[8,2]{1,0:T(8,128)S(1)} %copy.17.own.own_offsets.offsets, s32[8,2]{1,0:T(8,128)S(1)} %get-tuple-element.30.refs_0_.middle, s32[8,2]{1,0:T(8,128)S(1)} %collective-permute-done.far, f32[8,64,128]{2,1,0:T(8,128)S(1)} %get-tuple-element.39.refs_0_, ...), custom_call_target="tpu_custom_call" | custom-call | bytes 5242880 | tf_op jit(solution)/shard_map/pallas_call | solution.py:353
  79.7 0.0 collective-permute-done.7
  79.7 0.0 collective-permute-done.10.refs_0_
  79.7 0.3 collective-permute-done.11.refs_1_
  80.0 12.3 %all_to_all.10.parts = f32[8,9,8,128]{3,2,1,0:T(8,128)S(1)} all-to-all(f32[8,9,8,128]{3,2,1,0:T(8,128)S(1)} %add.3), channel_id=1, replica_groups={{0,2,4,6,8,10,12,14},{1,3,5,7,9,11,13,15},{16,18,20,22,24,26,28,30},{17..., dimensions={0} | all-to-all | bytes 589824 | tf_op jit(solution)/shard_map/all_to_all | solution.py:369
  92.4 11.3 %all_to_all.11.own = f32[8,8,8,128]{3,2,1,0:T(8,128)S(1)} all-to-all(f32[8,8,8,128]{3,2,1,0:T(8,128)S(1)} %shard_map.93), channel_id=1, replica_groups={{0,2,4,6,8,10,12,14},{1,3,5,7,9,11,13,15},{16,18,20,22,24,26,28,30},{17..., dimensions={0} | all-to-all | bytes 524288 | tf_op jit(solution)/shard_map/all_to_all | solution.py:377
  103.7 2.6 %collective-permute-start.12 = (f32[8,8,8,128]{3,2,1,0:T(8,128)S(1)}, f32[8,8,8,128]{3,2,1,0:T(8,128)S(1)}, u32[]{:S(2)}, u32[]{:S(2)}) collective-permute-start(f32[8,8,8,128]{3,2,1,0:T(8,128)S(1)} %all_to_all.11.own), channel_id=1, source_target_pairs={{0,1},{1,0},{2,3},{3,2},{4,5},{5,4},{6,7},{7,6},{8,9},{9,8},{10,11... | collective-permute-start | bytes 786440 | tf_op jit(solution)/shard_map/ppermute | solution.py:388
  106.3 3.6 %shard_map.92 = f32[4,64,2048]{2,1,0:T(8,128)} custom-call(s32[8,2]{1,0:T(8,128)S(1)} %copy.17.own.own_offsets.offsets, s32[8,2]{1,0:T(8,128)S(1)} %get-tuple-element.30.refs_0_.middle, s32[8,2]{1,0:T(8,128)S(1)} %collective-permute-done.far, f32[8,64,128]{2,1,0:T(8,128)S(1)} %collective-permute-done.10.refs_0_, ...), custom_call_target="tpu_custom_call", output_to_operand_aliasing={{}: (5, {})} | custom-call | bytes 5242880 | tf_op jit(solution)/shard_map/pallas_call | solution.py:353
  109.9 0.0 collective-permute-done.12.other
  109.9 1.5 %shard_map.94 = f32[8,128,128]{2,1,0:T(8,128)} custom-call(s32[8,2]{1,0:T(8,128)S(1)} %copy.17.own.own_offsets.offsets, f32[8,8,8,128]{3,2,1,0:T(8,128)S(1)} %all_to_all.11.own, f32[8,8,8,128]{3,2,1,0:T(8,128)S(1)} %collective-permute-done.12.other), custom_call_target="tpu_custom_call" | custom-call | tf_op jit(solution)/shard_map/pallas_call | solution.py:382
  (4 shorter events, 0.1 us)
Async XLA Ops:
  1.4 6.1 %collective-permute-start = (s32[8,2]{1,0:T(8,128)S(1)}, s32[8,2]{1,0:T(8,128)S(1)}, u32[]{:S(2)}, u32[]{:S(2)}) collective-permute-start(s32[8,2]{1,0:T(8,128)S(1)} %copy.17.own.own_offsets.offsets), channel_id=1, source_target_pairs={{0,2},{1,3},{2,4},{3,5},{4,6},{5,7},{6,8},{7,9},{8,10},{9,11},{10,... | collective-permute-start | bytes 200 | tf_op jit(solution)/shard_map/ppermute | solution.py:20
  7.5 1.6 %copy-start = (f32[2,2,64,2048]{3,2,1,0:T(8,128)S(1)}, f32[2,2,64,2048]{3,2,1,0:T(8,128)}, u32[]{:S(2)}) copy-start(f32[2,2,64,2048]{3,2,1,0:T(8,128)} %param.7) | copy-start | bytes 6291460
  9.1 1.0 copy-start.1
  10.1 6.5 %copy-start.4 = (f32[128,128]{1,0:T(8,128)S(1)}, f32[128,128]{1,0:T(8,128)}, u32[]{:S(2)}) copy-start(f32[128,128]{1,0:T(8,128)} %param.9) | copy-start | bytes 196612
  11.1 22.2 %copy-start.2 = (f32[4,2,128,128]{3,2,1,0:T(8,128)S(1)}, f32[4,2,128,128]{3,2,1,0:T(8,128)}, u32[]{:S(2)}) copy-start(f32[4,2,128,128]{3,2,1,0:T(8,128)} %refs_4_.3) | copy-start | bytes 1572868
  11.2 22.2 %copy-start.3 = (bf16[4,256,256]{2,1,0:T(8,128)(2,1)S(1)}, bf16[4,256,256]{2,1,0:T(8,128)(2,1)}, u32[]{:S(2)}) copy-start(bf16[4,256,256]{2,1,0:T(8,128)(2,1)} %constant.4.clone.refs_5_.refs_6_) | copy-start | bytes 1572868
  11.2 5.7 %collective-permute-start.1 = (f32[13,64,128]{2,1,0:T(8,128)S(1)}, f32[13,64,128]{2,1,0:T(8,128)S(1)}, u32[]{:S(2)}, u32[]{:S(2)}) collective-permute-start(f32[13,64,128]{2,1,0:T(8,128)S(1)} %get-tuple-element.26), channel_id=1, source_target_pairs={{0,1},{1,0},{2,3},{3,2},{4,5},{5,4},{6,7},{7,6},{8,9},{9,8},{10,11... | collective-permute-start | bytes 1277960 | tf_op jit(solution)/shard_map/ppermute | solution.py:311
  12.8 20.5 %collective-permute-start.2 = (f32[13,64,128]{2,1,0:T(8,128)S(1)}, f32[13,64,128]{2,1,0:T(8,128)S(1)}, u32[]{:S(2)}, u32[]{:S(2)}) collective-permute-start(f32[13,64,128]{2,1,0:T(8,128)S(1)} %get-tuple-element.27), channel_id=1, source_target_pairs={{0,15},{1,2},{2,1},{3,4},{4,3},{5,6},{6,5},{7,8},{8,7},{9,10},{10,... | collective-permute-start | bytes 1277960 | tf_op jit(solution)/shard_map/ppermute | solution.py:311
  14.4 28.4 %collective-permute-start.5 = (f32[24,64,128]{2,1,0:T(8,128)S(1)}, f32[24,64,128]{2,1,0:T(8,128)S(1)}, u32[]{:S(2)}, u32[]{:S(2)}) collective-permute-start(f32[24,64,128]{2,1,0:T(8,128)S(1)} %get-tuple-element.33), channel_id=1, source_target_pairs={{0,1},{1,0},{2,3},{3,2},{4,5},{5,4},{6,7},{7,6},{8,9},{9,8},{10,11... | collective-permute-start | bytes 2359304 | tf_op jit(solution)/shard_map/ppermute | solution.py:311
  16.6 26.2 %collective-permute-start.6 = (f32[24,64,128]{2,1,0:T(8,128)S(1)}, f32[24,64,128]{2,1,0:T(8,128)S(1)}, u32[]{:S(2)}, u32[]{:S(2)}) collective-permute-start(f32[24,64,128]{2,1,0:T(8,128)S(1)} %get-tuple-element.34), channel_id=1, source_target_pairs={{0,15},{1,2},{2,1},{3,4},{4,3},{5,6},{6,5},{7,8},{8,7},{9,10},{10,... | collective-permute-start | bytes 2359304 | tf_op jit(solution)/shard_map/ppermute | solution.py:311
  42.6 17.5 %collective-permute-start.3 = (f32[20,64,128]{2,1,0:T(8,128)S(1)}, f32[20,64,128]{2,1,0:T(8,128)S(1)}, u32[]{:S(2)}, u32[]{:S(2)}) collective-permute-start(f32[20,64,128]{2,1,0:T(8,128)S(1)} %get-tuple-element.31), channel_id=1, source_target_pairs={{0,1},{1,0},{2,3},{3,2},{4,5},{5,4},{6,7},{7,6},{8,9},{9,8},{10,11... | collective-permute-start | bytes 1966088 | tf_op jit(solution)/shard_map/ppermute | solution.py:311
  42.7 17.4 %collective-permute-start.4 = (f32[20,64,128]{2,1,0:T(8,128)S(1)}, f32[20,64,128]{2,1,0:T(8,128)S(1)}, u32[]{:S(2)}, u32[]{:S(2)}) collective-permute-start(f32[20,64,128]{2,1,0:T(8,128)S(1)} %get-tuple-element.32), channel_id=1, source_target_pairs={{0,15},{1,2},{2,1},{3,4},{4,3},{5,6},{6,5},{7,8},{8,7},{9,10},{10,... | collective-permute-start | bytes 1966088 | tf_op jit(solution)/shard_map/ppermute | solution.py:311
  58.0 13.0 %collective-permute-start.8 = (f32[16,64,128]{2,1,0:T(8,128)S(1)}, f32[16,64,128]{2,1,0:T(8,128)S(1)}, u32[]{:S(2)}, u32[]{:S(2)}) collective-permute-start(f32[16,64,128]{2,1,0:T(8,128)S(1)} %get-tuple-element.42), channel_id=1, source_target_pairs={{0,1},{1,0},{2,3},{3,2},{4,5},{5,4},{6,7},{7,6},{8,9},{9,8},{10,11... | collective-permute-start | bytes 1572872 | tf_op jit(solution)/shard_map/ppermute | solution.py:311
  60.1 14.6 %collective-permute-start.9 = (f32[16,64,128]{2,1,0:T(8,128)S(1)}, f32[16,64,128]{2,1,0:T(8,128)S(1)}, u32[]{:S(2)}, u32[]{:S(2)}) collective-permute-start(f32[16,64,128]{2,1,0:T(8,128)S(1)} %get-tuple-element.43), channel_id=1, source_target_pairs={{0,15},{1,2},{2,1},{3,4},{4,3},{5,6},{6,5},{7,8},{8,7},{9,10},{10,... | collective-permute-start | bytes 1572872 | tf_op jit(solution)/shard_map/ppermute | solution.py:311
  69.4 10.3 %collective-permute-start.7 = (f32[8,9,8,128]{3,2,1,0:T(8,128)S(1)}, f32[8,9,8,128]{3,2,1,0:T(8,128)S(1)}, u32[]{:S(2)}, u32[]{:S(2)}) collective-permute-start(f32[8,9,8,128]{3,2,1,0:T(8,128)S(1)} %get-tuple-element.38), channel_id=1, source_target_pairs={{0,1},{1,0},{2,3},{3,2},{4,5},{5,4},{6,7},{7,6},{8,9},{9,8},{10,11... | collective-permute-start | bytes 884744 | tf_op jit(solution)/shard_map/ppermute | solution.py:365
  71.0 8.8 %collective-permute-start.10 = (f32[8,64,128]{2,1,0:T(8,128)S(1)}, f32[8,64,128]{2,1,0:T(8,128)S(1)}, u32[]{:S(2)}, u32[]{:S(2)}) collective-permute-start(f32[8,64,128]{2,1,0:T(8,128)S(1)} %get-tuple-element.44), channel_id=1, source_target_pairs={{0,1},{1,0},{2,3},{3,2},{4,5},{5,4},{6,7},{7,6},{8,9},{9,8},{10,11... | collective-permute-start | bytes 786440 | tf_op jit(solution)/shard_map/ppermute | solution.py:311
  71.0 9.0 %collective-permute-start.11 = (f32[8,64,128]{2,1,0:T(8,128)S(1)}, f32[8,64,128]{2,1,0:T(8,128)S(1)}, u32[]{:S(2)}, u32[]{:S(2)}) collective-permute-start(f32[8,64,128]{2,1,0:T(8,128)S(1)} %get-tuple-element.45), channel_id=1, source_target_pairs={{0,15},{1,2},{2,1},{3,4},{4,3},{5,6},{6,5},{7,8},{8,7},{9,10},{10,... | collective-permute-start | bytes 786440 | tf_op jit(solution)/shard_map/ppermute | solution.py:311
  103.7 6.2 %collective-permute-start.12 = (f32[8,8,8,128]{3,2,1,0:T(8,128)S(1)}, f32[8,8,8,128]{3,2,1,0:T(8,128)S(1)}, u32[]{:S(2)}, u32[]{:S(2)}) collective-permute-start(f32[8,8,8,128]{3,2,1,0:T(8,128)S(1)} %all_to_all.11.own), channel_id=1, source_target_pairs={{0,1},{1,0},{2,3},{3,2},{4,5},{5,4},{6,7},{7,6},{8,9},{9,8},{10,11... | collective-permute-start | bytes 786440 | tf_op jit(solution)/shard_map/ppermute | solution.py:388
